TPU v7x, 32 devices: a whole 2x2x4 slice. The times are simulated.
32 devices in a mesh: pipe: 2 (over x), tensor: 4 (over y, core), dp: 4 (over z).
Axes of the slice: x: 2, y: 2, z: 4, core: 2. Of those that a mesh axis runs over, the one named last changes fastest.
Arguments:
- tokens: bfloat16 [4, 128, 4096], P('dp'), may hold values from -600 to 600
- norm_gains: float32 [2, 4096], P('pipe'), may hold values from 0.5 to 1.5
- qkv_weight: bfloat16 [2, 4096, 6144], P('pipe', 'dp', 'tensor'), may hold values from -0.1875 to 0.1875
- out_weight: bfloat16 [2, 4096, 4096], P('pipe', 'dp', 'tensor'), may hold values from -0.09375 to 0.09375
- cotangent: bfloat16 [4, 128, 4096], P('dp'), may hold values from -2.5 to 2.5
Outputs:
- qkv_grad: float32 [2, 4096, 6144], P('pipe', 'dp', 'tensor')
- out_grad: float32 [2, 4096, 4096], P('pipe', 'dp', 'tensor')
- gain_grad: float32 [2, 4096], P('pipe', 'dp')
All inputs are finite; a program needn't handle non-finite values.
Results may differ from a plain program's by a relative error of at most 0.025.
Values may be sent and summed in bfloat16 or wider, within the bound.
A program may use at most 128 MiB of HBM per device.

v0:
```python
import jax
import jax.numpy as jnp
from jax import lax
from jax.sharding import PartitionSpec as P

HD = 128
GROUP = 4
BLOCK = 32


EPSILON = 1e-05
HIGH = lax.Precision.HIGHEST


def from_behind(value, axis, steps):
    count = lax.axis_size(axis)
    leading, last = (max(0, -steps), min(count, count - steps))
    return lax.ppermute(value, axis, [(source, source + steps) for source in range(leading, last)])


def norm_parts(block_rows, gain_row):
    values = block_rows.astype(jnp.float32)
    recip_rms = lax.rsqrt(jnp.mean(values * values, axis=-1, keepdims=True) + EPSILON)
    normed = values * recip_rms
    return (normed, recip_rms, (normed * gain_row).astype(jnp.bfloat16))


def attend(query_rows, key_rows, value_rows, query_pos, key_pos):
    score_scale = query_rows.shape[-1] ** (-0.5)
    scores = (
        jnp.einsum("rgjd,cgd->gjrc", query_rows, key_rows, preferred_element_type=jnp.float32)
        * score_scale
    )
    allowed = key_pos[None, :] <= query_pos[:, None]
    scores = jnp.where(allowed, scores, -jnp.inf)
    row_max = jnp.max(scores, axis=-1, keepdims=True)
    raised = jnp.exp(scores - row_max)
    attn_probs = raised / jnp.sum(raised, axis=-1, keepdims=True)
    probs_low = attn_probs.astype(jnp.bfloat16)
    mixed_rows = jnp.einsum(
        "gjrc,cgd->rgjd", probs_low, value_rows, preferred_element_type=jnp.float32
    )
    return (attn_probs, probs_low, mixed_rows.astype(jnp.bfloat16))


def attend_back(query_rows, key_rows, value_rows, attn_probs, probs_low, grad_mixed):
    score_scale = query_rows.shape[-1] ** (-0.5)
    grad_low = jnp.einsum(
        "rgjd,cgd->gjrc", grad_mixed, value_rows, preferred_element_type=jnp.float32
    )
    inner_sum = jnp.sum(attn_probs * grad_low, axis=-1, keepdims=True)
    grad_score = attn_probs * (grad_low - inner_sum) * score_scale
    grad_query = jnp.einsum(
        "gjrc,cgd->rgjd", grad_score, key_rows.astype(jnp.float32), precision=HIGH
    )
    grad_key = jnp.einsum(
        "gjrc,rgjd->cgd", grad_score, query_rows.astype(jnp.float32), precision=HIGH
    )
    grad_value = jnp.einsum(
        "gjrc,rgjd->cgd", probs_low, grad_mixed, preferred_element_type=jnp.float32
    )
    return (grad_query, grad_key, grad_value)


def heads_total(partial_rows):
    return lax.psum(partial_rows.astype(jnp.bfloat16), "tensor").astype(jnp.float32)


def pass_section(block_value, offset):
    return from_behind(block_value, "pipe", offset)


def keep_active(active, fresh_state, old_state):
    return jax.tree.map(lambda fresh, old: jnp.where(active, fresh, old), fresh_state, old_state)


def shards(tokens, norm_gains, qkv_weight, out_weight, cotangent):
    sections = lax.axis_size("pipe")
    section_index = lax.axis_index("pipe")
    qkv_full, out_full = (
        lax.all_gather(qkv_weight, "dp", axis=1, tiled=True),
        lax.all_gather(out_weight, "dp", axis=1, tiled=True),
    )
    qkv_local = qkv_full[0]
    out_local = out_full[0]
    gain_row = norm_gains[0]
    tokens_local = tokens[0]
    grads_local = cotangent[0]
    seq_len = tokens_local.shape[0]
    model_width = tokens_local.shape[1]
    block_len = BLOCK
    blocks = seq_len // block_len
    proj_cols = qkv_local.shape[1]
    groups = proj_cols // ((GROUP + 2) * HD)
    head_cols = groups * GROUP * HD
    key_pos = jnp.arange(seq_len)
    contract_last = (((1,), (1,)), ((), ()))
    contract_rows = (((0,), (0,)), ((), ()))

    def forward_block(block_in, row_start, saved_state):
        saved_in, normed_all, query_all, key_cache, value_cache, mixed_all = saved_state
        normed, recip_rms, normed_low = norm_parts(block_in, gain_row)
        projected = jnp.dot(normed_low, qkv_local, preferred_element_type=jnp.float32).reshape(
            block_len, groups, GROUP + 2, HD
        )
        query_rows = projected[:, :, :GROUP].astype(jnp.bfloat16)
        key_new = projected[:, :, GROUP].astype(jnp.bfloat16)
        value_new = projected[:, :, GROUP + 1].astype(jnp.bfloat16)
        key_cache = lax.dynamic_update_slice_in_dim(key_cache, key_new, row_start, 0)
        value_cache = lax.dynamic_update_slice_in_dim(value_cache, value_new, row_start, 0)
        query_pos = row_start + jnp.arange(block_len)
        attn_probs, probs_low, mixed_rows = attend(
            query_rows, key_cache, value_cache, query_pos, key_pos
        )
        flat_mixed = mixed_rows.reshape(block_len, head_cols)
        partial_rows = lax.dot_general(
            flat_mixed, out_local, contract_last, preferred_element_type=jnp.float32
        )
        summed_heads = heads_total(partial_rows)
        block_out = (block_in.astype(jnp.float32) + summed_heads).astype(jnp.bfloat16)
        saved_in = lax.dynamic_update_slice_in_dim(saved_in, block_in, row_start, 0)
        normed_all = lax.dynamic_update_slice_in_dim(normed_all, normed_low, row_start, 0)
        query_all = lax.dynamic_update_slice_in_dim(query_all, query_rows, row_start, 0)
        mixed_all = lax.dynamic_update_slice_in_dim(mixed_all, flat_mixed, row_start, 0)
        return (block_out, (saved_in, normed_all, query_all, key_cache, value_cache, mixed_all))

    def forward_turn(turn_index, loop_carry):
        incoming, saved_state = loop_carry
        block_index = turn_index - section_index
        active = (block_index >= 0) & (block_index < blocks)
        row_start = jnp.clip(block_index, 0, blocks - 1) * block_len
        first_rows = lax.dynamic_slice_in_dim(tokens_local, row_start, block_len, 0)
        block_in = jnp.where(section_index == 0, first_rows, incoming)
        block_out, fresh_state = forward_block(block_in, row_start, saved_state)
        block_out = jnp.where(active, block_out, jnp.zeros_like(block_out))
        saved_state = keep_active(active, fresh_state, saved_state)
        return (pass_section(block_out, 1), saved_state)

    start_state = (
        jnp.zeros((seq_len, model_width), jnp.bfloat16),
        jnp.zeros((seq_len, model_width), jnp.bfloat16),
        jnp.zeros((seq_len, groups, GROUP, HD), jnp.bfloat16),
        jnp.zeros((seq_len, groups, HD), jnp.bfloat16),
        jnp.zeros((seq_len, groups, HD), jnp.bfloat16),
        jnp.zeros((seq_len, head_cols), jnp.bfloat16),
    )
    empty_block = jnp.zeros((block_len, model_width), jnp.bfloat16)
    last_block, saved_state = lax.fori_loop(
        0, blocks + sections - 1, forward_turn, (empty_block, start_state)
    )
    saved_in, normed_all, query_all, key_cache, value_cache, mixed_all = saved_state

    def backward_block(grad_in, row_start, grad_state):
        dkey_acc, dvalue_acc, dproj_all, grad_all, gain_acc = grad_state
        query_rows = lax.dynamic_slice_in_dim(query_all, row_start, block_len, 0)
        query_pos = row_start + jnp.arange(block_len)
        attn_probs, probs_low, unused_rows = attend(
            query_rows, key_cache, value_cache, query_pos, key_pos
        )
        grad_mixed = (
            jnp.dot(grad_in, out_local, preferred_element_type=jnp.float32)
            .astype(jnp.bfloat16)
            .reshape(block_len, groups, GROUP, HD)
        )
        grad_query, grad_key, grad_value = attend_back(
            query_rows, key_cache, value_cache, attn_probs, probs_low, grad_mixed
        )
        dkey_acc = dkey_acc + grad_key
        dvalue_acc = dvalue_acc + grad_value
        key_part = lax.dynamic_slice_in_dim(dkey_acc, row_start, block_len, 0).astype(jnp.bfloat16)
        value_part = lax.dynamic_slice_in_dim(dvalue_acc, row_start, block_len, 0).astype(
            jnp.bfloat16
        )
        grad_proj = jnp.concatenate(
            [grad_query.astype(jnp.bfloat16), key_part[:, :, None], value_part[:, :, None]], axis=2
        ).reshape(block_len, proj_cols)
        partial_rows = lax.dot_general(
            grad_proj, qkv_local, contract_last, preferred_element_type=jnp.float32
        )
        grad_normed = heads_total(partial_rows).astype(jnp.bfloat16)
        block_in = lax.dynamic_slice_in_dim(saved_in, row_start, block_len, 0)
        normed, recip_rms, normed_low = norm_parts(block_in, gain_row)
        grad_float = grad_normed.astype(jnp.float32)
        scaled = grad_float * gain_row
        grad_norm_in = recip_rms * (
            scaled - normed * jnp.mean(scaled * normed, axis=-1, keepdims=True)
        )
        block_out = (grad_in.astype(jnp.float32) + grad_norm_in).astype(jnp.bfloat16)
        gain_acc = gain_acc + jnp.sum(grad_float * normed, axis=0)
        dproj_all = lax.dynamic_update_slice_in_dim(dproj_all, grad_proj, row_start, 0)
        grad_all = lax.dynamic_update_slice_in_dim(grad_all, grad_in, row_start, 0)
        return (block_out, (dkey_acc, dvalue_acc, dproj_all, grad_all, gain_acc))

    def backward_turn(turn_index, loop_carry):
        incoming, grad_state = loop_carry
        block_index = blocks - 1 - turn_index + (sections - 1 - section_index)
        active = (block_index >= 0) & (block_index < blocks)
        row_start = jnp.clip(block_index, 0, blocks - 1) * block_len
        first_rows = lax.dynamic_slice_in_dim(grads_local, row_start, block_len, 0)
        grad_in = jnp.where(section_index == sections - 1, first_rows, incoming)
        block_out, fresh_state = backward_block(grad_in, row_start, grad_state)
        block_out = jnp.where(active, block_out, jnp.zeros_like(block_out))
        grad_state = keep_active(active, fresh_state, grad_state)
        return (pass_section(block_out, -1), grad_state)

    grad_start = (
        jnp.zeros((seq_len, groups, HD), jnp.float32),
        jnp.zeros((seq_len, groups, HD), jnp.float32),
        jnp.zeros((seq_len, proj_cols), jnp.bfloat16),
        jnp.zeros((seq_len, model_width), jnp.bfloat16),
        jnp.zeros((model_width,), jnp.float32),
    )
    last_grad, grad_state = lax.fori_loop(
        0, blocks + sections - 1, backward_turn, (empty_block, grad_start)
    )
    dkey_acc, dvalue_acc, dproj_all, grad_all, gain_acc = grad_state
    weight_part = lax.dot_general(
        normed_all, dproj_all, contract_rows, preferred_element_type=jnp.float32
    )
    output_part = lax.dot_general(
        grad_all, mixed_all, contract_rows, preferred_element_type=jnp.float32
    )
    qkv_result, out_result, gain_result = (
        lax.psum_scatter(
            weight_part[None].astype(jnp.bfloat16), "dp", scatter_dimension=1, tiled=True
        ).astype(jnp.float32),
        lax.psum_scatter(
            output_part[None].astype(jnp.bfloat16), "dp", scatter_dimension=1, tiled=True
        ).astype(jnp.float32),
        lax.psum_scatter(
            gain_acc[None].astype(jnp.bfloat16), "dp", scatter_dimension=1, tiled=True
        ).astype(jnp.float32),
    )
    return (qkv_result, out_result, gain_result)


def solution(mesh):
    in_specs = (
        P("dp", None, None),
        P("pipe", None),
        P("pipe", "dp", "tensor"),
        P("pipe", "dp", "tensor"),
        P("dp", None, None),
    )
    out_specs = (P("pipe", "dp", "tensor"), P("pipe", "dp", "tensor"), P("pipe", "dp"))
    return jax.shard_map(shards, mesh=mesh, in_specs=in_specs, out_specs=out_specs, check_vma=False)
```

profile of v0, /device:TPU:25, one launch (start us, length us, event | category | flops | bytes accessed | tf_op | source)
XLA Modules:
  0.0 1435.7 jit_solution(15629730317082416126)
XLA Ops:
  8.7 148.7 %all-gather.5.cloned.1.call-done = bf16[1,4096,1024]{2,1,0:T(8,128)(2,1)} async-done(((bf16[1,1024,1024]{2,1,0:T(8,128)(2,1)}), bf16[1,4096,1024]{2,1,0:T(8,128)(2,1)}) %all-gather.5.cloned.1.call-update) | async-done | bytes 8388624 | tf_op jit(solution)/shard_map/all_gather | solution.py:82
  157.4 218.0 %all-gather.3.cloned.1.call-done = bf16[1,4096,1536]{2,1,0:T(8,128)(2,1)} async-done(((bf16[1,1024,1536]{2,1,0:T(8,128)(2,1)}), bf16[1,4096,1536]{2,1,0:T(8,128)(2,1)}) %all-gather.3.cloned.1.call-update) | async-done | bytes 12582928 | tf_op jit(solution)/shard_map/all_gather | solution.py:81
  376.4 294.5 %while.53 = (s32[]{:T(128)}, bf16[32,4096]{1,0:T(8,128)(2,1)S(1)}, bf16[128,4096]{1,0:T(8,128)(2,1)S(1)}, bf16[128,4096]{1,0:T(8,128)(2,1)S(1)}, bf16[128,2,4,12...) while((s32[]{:T(128)}, bf16[32,4096]{1,0:T(8,128)(2,1)S(1)}, ...), condition=%wide.region_5.6_spmd.clone, body=%wide.region_0.5_spmd.clone.sunk | while | flops 690999872 | bytes 29994672 | solution.py:148
  377.7 6.9 convolution_convert_fusion.11
  386.1 6.6 convolution_convert_fusion.12
  393.4 31.4 %all-reduce.3.cloned.1.call-done = bf16[32,4096]{1,0:T(8,128)(2,1)} async-done(((bf16[32,4096]{1,0:T(8,128)(2,1)}), bf16[32,4096]{1,0:T(8,128)(2,1)}) %all-reduce.3.cloned.1.call-update) | async-done | bytes 262160 | tf_op jit(solution)/shard_map/while/body/eval_jaxpr/psum | solution.py:66
  425.9 3.1 collective-permute-start
  434.1 6.9 convolution_convert_fusion.11
  443.3 6.6 convolution_convert_fusion.12
  450.6 33.7 %all-reduce.3.cloned.1.call-done = bf16[32,4096]{1,0:T(8,128)(2,1)} async-done(((bf16[32,4096]{1,0:T(8,128)(2,1)}), bf16[32,4096]{1,0:T(8,128)(2,1)}) %all-reduce.3.cloned.1.call-update) | async-done | bytes 262160 | tf_op jit(solution)/shard_map/while/body/eval_jaxpr/psum | solution.py:66
  485.5 3.1 collective-permute-start
  493.6 6.9 convolution_convert_fusion.11
  502.8 6.6 convolution_convert_fusion.12
  510.1 33.7 %all-reduce.3.cloned.1.call-done = bf16[32,4096]{1,0:T(8,128)(2,1)} async-done(((bf16[32,4096]{1,0:T(8,128)(2,1)}), bf16[32,4096]{1,0:T(8,128)(2,1)}) %all-reduce.3.cloned.1.call-update) | async-done | bytes 262160 | tf_op jit(solution)/shard_map/while/body/eval_jaxpr/psum | solution.py:66
  545.0 3.1 collective-permute-start
  553.1 6.9 convolution_convert_fusion.11
  562.3 6.6 convolution_convert_fusion.12
  569.7 33.7 %all-reduce.3.cloned.1.call-done = bf16[32,4096]{1,0:T(8,128)(2,1)} async-done(((bf16[32,4096]{1,0:T(8,128)(2,1)}), bf16[32,4096]{1,0:T(8,128)(2,1)}) %all-reduce.3.cloned.1.call-update) | async-done | bytes 262160 | tf_op jit(solution)/shard_map/while/body/eval_jaxpr/psum | solution.py:66
  604.5 3.1 collective-permute-start
  612.6 6.9 convolution_convert_fusion.11
  621.9 6.6 convolution_convert_fusion.12
  629.2 33.7 %all-reduce.3.cloned.1.call-done = bf16[32,4096]{1,0:T(8,128)(2,1)} async-done(((bf16[32,4096]{1,0:T(8,128)(2,1)}), bf16[32,4096]{1,0:T(8,128)(2,1)}) %all-reduce.3.cloned.1.call-update) | async-done | bytes 262160 | tf_op jit(solution)/shard_map/while/body/eval_jaxpr/psum | solution.py:66
  664.0 3.1 collective-permute-start
  672.5 358.5 %while.54 = (s32[]{:T(128)}, bf16[32,4096]{1,0:T(8,128)(2,1)}, f32[128,2,128]{2,0,1:T(8,128)}, f32[128,2,128]{2,0,1:T(8,128)}, bf16[128,1536]{1,0:T(8,128)(2,1)}...) while((s32[]{:T(128)}, bf16[32,4096]{1,0:T(8,128)(2,1)}, ...), condition=%wide.region_14.15_spmd.clone, body=%wide.region_6.14_spmd.clone.sunk | while | flops 809857280 | bytes 32129012 | solution.py:213
  673.7 4.9 convolution_convert_fusion.13
  683.6 2.0 select_select_fusion.4
  685.6 2.1 select_select_fusion.5
  690.3 9.0 convolution_convert_fusion.14
  700.0 33.6 %all-reduce.5.cloned.1.call-done = bf16[32,4096]{1,0:T(8,128)(2,1)} async-done(((bf16[32,4096]{1,0:T(8,128)(2,1)}), bf16[32,4096]{1,0:T(8,128)(2,1)}) %all-reduce.5.cloned.1.call-update) | async-done | bytes 262160 | tf_op jit(solution)/shard_map/while/body/eval_jaxpr/psum | solution.py:66
  734.9 1.9 fusion.156
  739.6 5.2 collective-permute-done.1
  746.7 4.9 convolution_convert_fusion.13
  756.6 2.1 select_select_fusion.4
  758.7 2.3 select_select_fusion.5
  763.5 9.0 convolution_convert_fusion.14
  773.2 31.7 %all-reduce.5.cloned.1.call-done = bf16[32,4096]{1,0:T(8,128)(2,1)} async-done(((bf16[32,4096]{1,0:T(8,128)(2,1)}), bf16[32,4096]{1,0:T(8,128)(2,1)}) %all-reduce.5.cloned.1.call-update) | async-done | bytes 262160 | tf_op jit(solution)/shard_map/while/body/eval_jaxpr/psum | solution.py:66
  806.3 1.9 fusion.156
  811.0 5.2 collective-permute-done.1
  818.1 4.9 convolution_convert_fusion.13
  828.0 2.1 select_select_fusion.4
  830.1 2.3 select_select_fusion.5
  834.8 9.0 convolution_convert_fusion.14
  844.6 31.7 %all-reduce.5.cloned.1.call-done = bf16[32,4096]{1,0:T(8,128)(2,1)} async-done(((bf16[32,4096]{1,0:T(8,128)(2,1)}), bf16[32,4096]{1,0:T(8,128)(2,1)}) %all-reduce.5.cloned.1.call-update) | async-done | bytes 262160 | tf_op jit(solution)/shard_map/while/body/eval_jaxpr/psum | solution.py:66
  877.6 1.9 fusion.156
  882.4 5.2 collective-permute-done.1
  889.4 4.9 convolution_convert_fusion.13
  899.3 2.1 select_select_fusion.4
  901.4 2.3 select_select_fusion.5
  906.2 9.0 convolution_convert_fusion.14
  915.9 31.7 %all-reduce.5.cloned.1.call-done = bf16[32,4096]{1,0:T(8,128)(2,1)} async-done(((bf16[32,4096]{1,0:T(8,128)(2,1)}), bf16[32,4096]{1,0:T(8,128)(2,1)}) %all-reduce.5.cloned.1.call-update) | async-done | bytes 262160 | tf_op jit(solution)/shard_map/while/body/eval_jaxpr/psum | solution.py:66
  953.7 5.2 collective-permute-done.1
  960.8 4.9 convolution_convert_fusion.13
  970.7 2.1 select_select_fusion.4
  972.8 2.3 select_select_fusion.5
  977.6 9.0 convolution_convert_fusion.14
  987.3 31.7 %all-reduce.5.cloned.1.call-done = bf16[32,4096]{1,0:T(8,128)(2,1)} async-done(((bf16[32,4096]{1,0:T(8,128)(2,1)}), bf16[32,4096]{1,0:T(8,128)(2,1)}) %all-reduce.5.cloned.1.call-update) | async-done | bytes 262160 | tf_op jit(solution)/shard_map/while/body/eval_jaxpr/psum | solution.py:66
  1025.1 5.2 collective-permute-done.1
  1033.6 6.6 convert_bitcast_fusion
  1040.2 6.4 fusion.74
  1046.7 14.4 %reduce-scatter.10.cloned.1.call-done = bf16[1024,1]{1,0:T(8,128)(2,1)} async-done(((bf16[4096,1]{1,0:T(8,128)(2,1)}), bf16[1024,1]{1,0:T(8,128)(2,1)}) %reduce-scatter.10.cloned.1.call-update) | async-done | bytes 2064
  1062.8 145.7 %reduce-scatter.8.cloned.1.call-done = bf16[1,1024,1024]{2,1,0:T(8,128)(2,1)} async-done(((bf16[1,4096,1024]{2,1,0:T(8,128)(2,1)}), bf16[1,1024,1024]{2,1,0:T(8,128)(2,1)}) %reduce-scatter.8.cloned.1.call-update) | async-done | bytes 2097168 | tf_op jit(solution)/shard_map/reduce_scatter | solution.py:227
  1208.5 4.1 convert_element_type.221
  1212.6 211.2 %reduce-scatter.6.cloned.1.call-done = bf16[1,1024,1536]{2,1,0:T(8,128)(2,1)} async-done(((bf16[1,4096,1536]{2,1,0:T(8,128)(2,1)}), bf16[1,1024,1536]{2,1,0:T(8,128)(2,1)}) %reduce-scatter.6.cloned.1.call-update) | async-done | bytes 3145744 | tf_op jit(solution)/shard_map/reduce_scatter | solution.py:224
  1423.8 5.5 convert_element_type.218
  (333 shorter events, 127.1 us)
Async XLA Ops:
  7.2 150.2 %all-gather.5.cloned.1.call-start = ((), (), s32[]{:S(2)}) async-start(), calls=%async_computation.4 | async-start | bytes 10485760 | tf_op jit(solution)/shard_map/all_gather | solution.py:82
  7.9 367.5 %all-gather.3.cloned.1.call-start = ((), (), s32[]{:S(2)}) async-start(), calls=%async_computation.3 | async-start | bytes 15728640 | tf_op jit(solution)/shard_map/all_gather | solution.py:81
  376.4 48.4 %all-reduce.3.cloned.1.call-start = ((), (), s32[]{:S(2)}) async-start(), calls=%async_computation.8 | async-start | bytes 524288 | tf_op jit(solution)/shard_map/while/body/eval_jaxpr/psum | solution.py:66
  384.7 40.1 %copy-start = (f32[1,4096]{1,0:T(1,128)S(1)}, f32[1,4096]{1,0:T(1,128)}, u32[]{:S(2)}) copy-start(f32[1,4096]{1,0:T(1,128)} %get-tuple-element.1168) | copy-start | bytes 49156 | tf_op jit(solution)/shard_map/while
  425.9 6.9 collective-permute-start
  432.8 51.5 %all-reduce.3.cloned.1.call-start = ((), (), s32[]{:S(2)}) async-start(), calls=%async_computation.8 | async-start | bytes 524288 | tf_op jit(solution)/shard_map/while/body/eval_jaxpr/psum | solution.py:66
  441.0 43.3 %copy-start = (f32[1,4096]{1,0:T(1,128)S(1)}, f32[1,4096]{1,0:T(1,128)}, u32[]{:S(2)}) copy-start(f32[1,4096]{1,0:T(1,128)} %get-tuple-element.1168) | copy-start | bytes 49156 | tf_op jit(solution)/shard_map/while
  485.5 6.9 collective-permute-start
  492.3 51.5 %all-reduce.3.cloned.1.call-start = ((), (), s32[]{:S(2)}) async-start(), calls=%async_computation.8 | async-start | bytes 524288 | tf_op jit(solution)/shard_map/while/body/eval_jaxpr/psum | solution.py:66
  500.5 43.3 %copy-start = (f32[1,4096]{1,0:T(1,128)S(1)}, f32[1,4096]{1,0:T(1,128)}, u32[]{:S(2)}) copy-start(f32[1,4096]{1,0:T(1,128)} %get-tuple-element.1168) | copy-start | bytes 49156 | tf_op jit(solution)/shard_map/while
  545.0 6.9 collective-permute-start
  551.9 51.5 %all-reduce.3.cloned.1.call-start = ((), (), s32[]{:S(2)}) async-start(), calls=%async_computation.8 | async-start | bytes 524288 | tf_op jit(solution)/shard_map/while/body/eval_jaxpr/psum | solution.py:66
  560.0 43.3 %copy-start = (f32[1,4096]{1,0:T(1,128)S(1)}, f32[1,4096]{1,0:T(1,128)}, u32[]{:S(2)}) copy-start(f32[1,4096]{1,0:T(1,128)} %get-tuple-element.1168) | copy-start | bytes 49156 | tf_op jit(solution)/shard_map/while
  604.5 6.9 collective-permute-start
  611.4 51.5 %all-reduce.3.cloned.1.call-start = ((), (), s32[]{:S(2)}) async-start(), calls=%async_computation.8 | async-start | bytes 524288 | tf_op jit(solution)/shard_map/while/body/eval_jaxpr/psum | solution.py:66
  619.6 43.3 %copy-start = (f32[1,4096]{1,0:T(1,128)S(1)}, f32[1,4096]{1,0:T(1,128)}, u32[]{:S(2)}) copy-start(f32[1,4096]{1,0:T(1,128)} %get-tuple-element.1168) | copy-start | bytes 49156 | tf_op jit(solution)/shard_map/while
  664.0 6.9 collective-permute-start
  670.9 1.6 copy-start.4
  672.5 61.1 %all-reduce.5.cloned.1.call-start = ((), (), s32[]{:S(2)}) async-start(), calls=%async_computation.9 | async-start | bytes 524288 | tf_op jit(solution)/shard_map/while/body/eval_jaxpr/psum | solution.py:66
  678.7 1.8 copy-start.7
  680.5 0.6 copy-start.8
  682.4 51.3 %copy-start.1 = (f32[1,4096]{1,0:T(1,128)S(1)}, f32[1,4096]{1,0:T(1,128)}, u32[]{:S(2)}) copy-start(f32[1,4096]{1,0:T(1,128)} %get-tuple-element.1239) | copy-start | bytes 49156 | tf_op jit(solution)/shard_map/while
  687.8 51.9 %copy-start.5 = (f32[4096]{0:T(1024)S(1)}, f32[4096]{0:T(1024)}, u32[]{:S(2)}) copy-start(f32[4096]{0:T(1024)} %get-tuple-element.1206) | copy-start | bytes 49156 | tf_op jit(solution)/shard_map/while
  736.8 8.1 collective-permute-start.1
  739.6 5.2 copy-start.6
  744.9 0.7 copy-start.2
  745.6 59.4 %all-reduce.5.cloned.1.call-start = ((), (), s32[]{:S(2)}) async-start(), calls=%async_computation.9 | async-start | bytes 524288 | tf_op jit(solution)/shard_map/while/body/eval_jaxpr/psum | solution.py:66
  751.8 1.8 copy-start.7
  753.6 0.6 copy-start.8
  755.4 49.6 %copy-start.1 = (f32[1,4096]{1,0:T(1,128)S(1)}, f32[1,4096]{1,0:T(1,128)}, u32[]{:S(2)}) copy-start(f32[1,4096]{1,0:T(1,128)} %get-tuple-element.1239) | copy-start | bytes 49156 | tf_op jit(solution)/shard_map/while
  761.0 50.0 %copy-start.5 = (f32[4096]{0:T(1024)S(1)}, f32[4096]{0:T(1024)}, u32[]{:S(2)}) copy-start(f32[4096]{0:T(1024)} %get-tuple-element.1206) | copy-start | bytes 49156 | tf_op jit(solution)/shard_map/while
  808.1 8.1 collective-permute-start.1
  811.0 5.2 copy-start.6
  816.2 0.7 copy-start.2
  816.9 59.4 %all-reduce.5.cloned.1.call-start = ((), (), s32[]{:S(2)}) async-start(), calls=%async_computation.9 | async-start | bytes 524288 | tf_op jit(solution)/shard_map/while/body/eval_jaxpr/psum | solution.py:66
  823.1 1.8 copy-start.7
  824.9 0.6 copy-start.8
  826.7 49.6 %copy-start.1 = (f32[1,4096]{1,0:T(1,128)S(1)}, f32[1,4096]{1,0:T(1,128)}, u32[]{:S(2)}) copy-start(f32[1,4096]{1,0:T(1,128)} %get-tuple-element.1239) | copy-start | bytes 49156 | tf_op jit(solution)/shard_map/while
  832.3 50.0 %copy-start.5 = (f32[4096]{0:T(1024)S(1)}, f32[4096]{0:T(1024)}, u32[]{:S(2)}) copy-start(f32[4096]{0:T(1024)} %get-tuple-element.1206) | copy-start | bytes 49156 | tf_op jit(solution)/shard_map/while
  879.5 8.1 collective-permute-start.1
  882.4 5.2 copy-start.6
  887.6 0.7 copy-start.2
  888.3 59.4 %all-reduce.5.cloned.1.call-start = ((), (), s32[]{:S(2)}) async-start(), calls=%async_computation.9 | async-start | bytes 524288 | tf_op jit(solution)/shard_map/while/body/eval_jaxpr/psum | solution.py:66
  894.5 1.8 copy-start.7
  896.3 0.6 copy-start.8
  898.1 49.6 %copy-start.1 = (f32[1,4096]{1,0:T(1,128)S(1)}, f32[1,4096]{1,0:T(1,128)}, u32[]{:S(2)}) copy-start(f32[1,4096]{1,0:T(1,128)} %get-tuple-element.1239) | copy-start | bytes 49156 | tf_op jit(solution)/shard_map/while
  903.7 50.0 %copy-start.5 = (f32[4096]{0:T(1024)S(1)}, f32[4096]{0:T(1024)}, u32[]{:S(2)}) copy-start(f32[4096]{0:T(1024)} %get-tuple-element.1206) | copy-start | bytes 49156 | tf_op jit(solution)/shard_map/while
  950.9 8.1 collective-permute-start.1
  953.7 5.2 copy-start.6
  958.9 0.7 copy-start.2
  959.6 59.4 %all-reduce.5.cloned.1.call-start = ((), (), s32[]{:S(2)}) async-start(), calls=%async_computation.9 | async-start | bytes 524288 | tf_op jit(solution)/shard_map/while/body/eval_jaxpr/psum | solution.py:66
  965.8 1.8 copy-start.7
  967.6 0.6 copy-start.8
  969.5 49.6 %copy-start.1 = (f32[1,4096]{1,0:T(1,128)S(1)}, f32[1,4096]{1,0:T(1,128)}, u32[]{:S(2)}) copy-start(f32[1,4096]{1,0:T(1,128)} %get-tuple-element.1239) | copy-start | bytes 49156 | tf_op jit(solution)/shard_map/while
  975.1 50.0 %copy-start.5 = (f32[4096]{0:T(1024)S(1)}, f32[4096]{0:T(1024)}, u32[]{:S(2)}) copy-start(f32[4096]{0:T(1024)} %get-tuple-element.1206) | copy-start | bytes 49156 | tf_op jit(solution)/shard_map/while
  1022.2 8.1 collective-permute-start.1
  1025.1 5.2 copy-start.6
  1030.3 0.7 copy-start.2
  1031.0 30.1 %reduce-scatter.10.cloned.1.call-start = ((), (), s32[]{:S(2)}) async-start(), calls=%async_computation.7 | async-start | bytes 1310720
  1033.3 175.2 %reduce-scatter.8.cloned.1.call-start = ((), (), s32[]{:S(2)}) async-start(), calls=%async_computation.6 | async-start | bytes 10485760 | tf_op jit(solution)/shard_map/reduce_scatter | solution.py:227
  1033.6 6.7 copy-start.3
  1040.2 383.6 %reduce-scatter.6.cloned.1.call-start = ((), (), s32[]{:S(2)}) async-start(), calls=%async_computation.5 | async-start | bytes 15728640 | tf_op jit(solution)/shard_map/reduce_scatter | solution.py:224
Sparse Core Ops, SparseCore 0:
  9.6 147.7 all-gather.4
  159.0 216.3 all-gather.2
  392.9 31.8 all-reduce.2
  450.1 34.1 all-reduce.2
  509.6 34.1 all-reduce.2
  569.1 34.1 all-reduce.2
  628.6 34.1 all-reduce.2
  699.4 34.1 all-reduce.4
  772.6 32.2 all-reduce.4
  844.0 32.2 all-reduce.4
  915.4 32.2 all-reduce.4
  986.7 32.2 all-reduce.4
  1034.7 26.3 reduce-scatter.9
  1063.4 145.0 reduce-scatter.7
  1210.8 212.8 reduce-scatter.5
where the time goes:
time: 1440 us
  waiting for transfers between devices  1100 us (76%)
  matrix products  197 us (14%)
  other arithmetic  75 us (5%)
  local copies, waits for them, and re-layouts  26 us (2%)
  starting transfers between devices  22.4 us (2%)
    psum x10, waiting for transfers between devices, heads_total(): lax.psum(partial_rows.astype(jnp.bfloat16), 'tensor').astype(jnp.float32)  327 us
    all_gather x1, waiting for transfers between devices, shards(): lax.all_gather(qkv_weight, 'dp', axis=1, tiled=True)  218 us
    reduce_scatter x1, waiting for transfers between devices, shards(): lax.psum_scatter(weight_part[None].astype(jnp.bfloat16), 'dp', scatter_di...  211 us
    all_gather x1, waiting for transfers between devices, shards(): lax.all_gather(out_weight, 'dp', axis=1, tiled=True)  149 us
    reduce_scatter x1, waiting for transfers between devices, shards(): lax.psum_scatter(output_part[None].astype(jnp.bfloat16), 'dp', scatter_di...  146 us
    dot_general x5, matrix products, backward_block(): lax.dot_general(grad_proj, qkv_local, contract_last, preferred_element_ty...  45.1 us
    select_n x45, other arithmetic, keep_active(): jnp.where(active, fresh, old)  38.5 us
    dot_general x5, matrix products, forward_block(): jnp.dot(normed_low, qkv_local, preferred_element_type=jnp.float32)  34.6 us
  transfers between devices with their start and end apart: 25, of which 25 were waited for; matrix products, arithmetic and copies ran while one was open for 3% of the time, Pallas kernels for 0%

commit v1 on v0

v1 whole, which is shorter than its diff:
```python
import functools

import jax
import jax.numpy as jnp
from jax import lax
from jax.experimental import pallas as pl
from jax.experimental.pallas import tpu as pltpu
from jax.sharding import PartitionSpec as P

HD = 128
GROUP = 4
EPSILON = 1e-05
BF = jnp.bfloat16
F32 = jnp.float32
MESH = pl.DeviceIdType.MESH
KERNELS = True


def dot(a, b, ca, cb):
    return lax.dot_general(a, b, (((ca,), (cb,)), ((), ())), preferred_element_type=F32)


def exchange_kernel(axis, spread, count, *refs):
    arrays = len(spread)
    ins, outs = refs[:arrays], refs[arrays : 2 * arrays]
    send_sems, recv_sems, own_sems = refs[2 * arrays :]
    me = lax.axis_index(axis)
    barrier = pltpu.get_barrier_semaphore()
    for step in range(1, count):
        peer = lax.rem(me + step, count)
        pl.semaphore_signal(barrier, inc=1, device_id={axis: peer}, device_id_type=MESH)
    own = []
    for index in range(arrays):
        block = ins[index].at[me] if spread[index] else ins[index]
        copy = pltpu.make_async_copy(block, outs[index].at[me], own_sems.at[index])
        copy.start()
        own.append(copy)
    pl.semaphore_wait(barrier, count - 1)
    sent = []
    for step in range(1, count):
        peer = lax.rem(me + step, count)
        for index in range(arrays):
            copy = pltpu.make_async_remote_copy(
                src_ref=ins[index].at[peer] if spread[index] else ins[index],
                dst_ref=outs[index].at[me],
                send_sem=send_sems.at[index, step],
                recv_sem=recv_sems.at[index, step],
                device_id={axis: peer},
                device_id_type=MESH,
            )
            copy.start()
            sent.append(copy)
    for copy in own:
        copy.wait()
    for copy in sent:
        copy.wait()


def exchange(axis, arrays, spread, collective_id):
    if not KERNELS:
        return [
            lax.all_to_all(a, axis, 0, 0) if s else lax.all_gather(a, axis) for a, s in zip(arrays, spread)
        ]
    count = lax.axis_size(axis)
    shapes = [a.shape if s else (count, *a.shape) for a, s in zip(arrays, spread)]
    vmem = pl.BlockSpec(memory_space=pltpu.VMEM)
    return pl.pallas_call(
        functools.partial(exchange_kernel, axis, spread, count),
        out_shape=[jax.ShapeDtypeStruct(s, a.dtype) for s, a in zip(shapes, arrays)],
        in_specs=[vmem] * len(arrays),
        out_specs=[vmem] * len(arrays),
        scratch_shapes=[
            pltpu.SemaphoreType.DMA((len(arrays), count)),
            pltpu.SemaphoreType.DMA((len(arrays), count)),
            pltpu.SemaphoreType.DMA((len(arrays),)),
        ],
        compiler_params=pltpu.CompilerParams(
            collective_id=collective_id, has_side_effects=True, vmem_limit_bytes=48 << 20
        ),
    )(*arrays)


def relay_kernel(count, part_ref, rest_ref, out_ref, landed, own, passed, sems, pipe_sems, gather_sems):
    tensor = lax.axis_index("tensor")
    other = 1 - lax.axis_index("pipe")
    barrier = pltpu.get_barrier_semaphore()
    for step in range(1, count):
        peer = lax.rem(tensor + step, count)
        pl.semaphore_signal(barrier, inc=1, device_id={"tensor": peer}, device_id_type=MESH)
    pl.semaphore_signal(barrier, inc=1, device_id={"pipe": other}, device_id_type=MESH)
    pl.semaphore_wait(barrier, count)
    copies = []
    for step in range(1, count):
        peer = lax.rem(tensor + step, count)
        copy = pltpu.make_async_remote_copy(
            src_ref=part_ref.at[peer],
            dst_ref=landed.at[step],
            send_sem=sems.at[0, step],
            recv_sem=sems.at[1, step],
            device_id={"tensor": peer},
            device_id_type=MESH,
        )
        copy.start()
        copies.append(copy)
    total = rest_ref[...].astype(F32) + part_ref[tensor].astype(F32)
    for step, copy in enumerate(copies, 1):
        copy.wait_recv()
        total = total + landed[step].astype(F32)
    own[...] = total.astype(BF)
    across = pltpu.make_async_remote_copy(
        src_ref=own,
        dst_ref=passed,
        send_sem=pipe_sems.at[0],
        recv_sem=pipe_sems.at[1],
        device_id={"pipe": other},
        device_id_type=MESH,
    )
    across.start()
    across.wait_recv()
    spread = []
    for step in range(1, count):
        peer = lax.rem(tensor + step, count)
        copy = pltpu.make_async_remote_copy(
            src_ref=passed,
            dst_ref=out_ref.at[tensor],
            send_sem=gather_sems.at[0, step],
            recv_sem=gather_sems.at[1, step],
            device_id={"tensor": peer},
            device_id_type=MESH,
        )
        copy.start()
        spread.append(copy)
    out_ref[tensor] = passed[...]
    for copy in copies:
        copy.wait_send()
    across.wait_send()
    for copy in spread:
        copy.wait()


def relay(parts, rest, collective_id):
    count = lax.axis_size("tensor")
    rows, width = parts.shape[0] // count, parts.shape[1]
    parts = parts.reshape(count, rows, width)
    own = lax.dynamic_index_in_dim(rest.reshape(count, rows, width), lax.axis_index("tensor"), 0, False)
    if not KERNELS:
        summed = lax.psum_scatter(parts, "tensor", scatter_dimension=0, tiled=False).astype(F32)
        passed = lax.ppermute((own.astype(F32) + summed).astype(BF), "pipe", [(0, 1), (1, 0)])
        return lax.all_gather(passed, "tensor").reshape(count * rows, width)
    vmem = pl.BlockSpec(memory_space=pltpu.VMEM)
    out = pl.pallas_call(
        functools.partial(relay_kernel, count),
        out_shape=jax.ShapeDtypeStruct(parts.shape, BF),
        in_specs=[vmem] * 2,
        out_specs=vmem,
        scratch_shapes=[
            pltpu.VMEM(parts.shape, BF),
            pltpu.VMEM((rows, width), BF),
            pltpu.VMEM((rows, width), BF),
            pltpu.SemaphoreType.DMA((2, count)),
            pltpu.SemaphoreType.DMA((2,)),
            pltpu.SemaphoreType.DMA((2, count)),
        ],
        compiler_params=pltpu.CompilerParams(
            collective_id=collective_id, has_side_effects=True, vmem_limit_bytes=48 << 20
        ),
    )(parts, own)
    return out.reshape(count * rows, width)


def split_heads(flat, seq, groups, count):
    return jnp.transpose(flat.reshape(seq, groups, count, HD), (1, 2, 0, 3))


def attend(proj, seq, groups):
    heads = split_heads(proj, seq, groups, GROUP + 2)
    query = heads[:, :GROUP].reshape(groups, GROUP * seq, HD)
    key, value = heads[:, GROUP], heads[:, GROUP + 1]
    scores = jnp.einsum("grd,gcd->grc", query, key, preferred_element_type=F32) * HD**-0.5
    scores = scores.reshape(groups, GROUP, seq, seq)
    scores = jnp.where(jnp.tri(seq, dtype=bool), scores, -jnp.inf)
    raised = jnp.exp(scores - jnp.max(scores, axis=-1, keepdims=True))
    probs = (raised / jnp.sum(raised, axis=-1, keepdims=True)).reshape(groups, GROUP * seq, seq)
    mixed = jnp.einsum("grc,gcd->grd", probs.astype(BF), value, preferred_element_type=F32)
    mixed = mixed.astype(BF).reshape(groups, GROUP, seq, HD)
    return query, key, value, probs, jnp.transpose(mixed, (2, 0, 1, 3)).reshape(seq, groups * GROUP * HD)


def attend_back(query, key, value, probs, grad_mixed, seq, groups):
    grad = split_heads(grad_mixed, seq, groups, GROUP).reshape(groups, GROUP * seq, HD)
    grad_low = jnp.einsum("grd,gcd->grc", grad, value, preferred_element_type=F32)
    inner = jnp.sum(probs * grad_low, axis=-1, keepdims=True)
    grad_score = (probs * (grad_low - inner) * HD**-0.5).astype(BF)
    grad_query = jnp.einsum("grc,gcd->grd", grad_score, key, preferred_element_type=F32)
    grad_key = jnp.einsum("grc,grd->gcd", grad_score, query, preferred_element_type=F32)
    grad_value = jnp.einsum("grc,grd->gcd", probs.astype(BF), grad, preferred_element_type=F32)
    heads = jnp.concatenate(
        [grad_query.reshape(groups, GROUP, seq, HD), grad_key[:, None], grad_value[:, None]], axis=1
    )
    return jnp.transpose(heads, (2, 0, 1, 3)).reshape(seq, groups * (GROUP + 2) * HD)


def shards(tokens, norm_gains, qkv_weight, out_weight, cotangent):
    first = lax.axis_index("pipe") == 0
    count = lax.axis_size("dp")
    qkv, out = qkv_weight[0], out_weight[0]
    width, cols = qkv.shape
    head_cols = out.shape[1]
    seq, model = tokens.shape[1:]
    rows = count * seq
    groups = cols // ((GROUP + 2) * HD)
    gain = lax.dynamic_slice_in_dim(norm_gains[0], lax.axis_index("dp") * width, width, 0)[None]

    def project(block):
        scaled = block.astype(F32)
        squares = jnp.sum(scaled * scaled, axis=-1).reshape(count, 1, seq)
        squares = jnp.broadcast_to(squares, (count, 8, seq))
        return dot((scaled * gain).astype(BF), qkv, 1, 0).astype(BF), squares

    def summed(slots):
        return jnp.sum(slots.astype(F32), axis=0)

    held = jnp.where(first, tokens[0], cotangent[0])
    held = jnp.transpose(held.reshape(seq, count, width), (1, 0, 2))
    (held,) = exchange("dp", [held], [True], 0)
    held = held.reshape(rows, width)

    proj_part, squares = project(held)
    mixed_part = dot(held, out, 1, 0).astype(BF)
    mixed_part = jnp.pad(mixed_part, ((0, 0), (0, cols - head_cols)))
    part = jnp.where(first, proj_part, mixed_part).reshape(count, seq, cols)
    part, squares = exchange("dp", [part, squares], [True, True], 1)
    raw_start = summed(part)
    squares_start = summed(squares)[0]
    recip = lax.rsqrt(squares_start / model + EPSILON)[:, None]
    grad_mixed_start = raw_start[:, :head_cols].astype(BF)
    mixed = attend((raw_start * recip).astype(BF), seq, groups)[-1]
    (mixed_start,) = exchange("dp", [mixed], [False], 2)
    mixed_start = mixed_start.reshape(rows, head_cols)
    carried = relay(dot(mixed_start, out, 1, 1).astype(BF), held, 3)

    part, squares = project(carried)
    part, squares = exchange("dp", [part.reshape(count, seq, cols), squares], [True, True], 4)
    raw_next = summed(part)
    raw = jnp.where(first, raw_start, raw_next)
    recip = lax.rsqrt(jnp.where(first, squares_start, summed(squares)[0]) / model + EPSILON)[:, None]
    query, key, value, probs, mixed = attend((raw * recip).astype(BF), seq, groups)
    grad_proj = attend_back(query, key, value, probs, grad_mixed_start, seq, groups)
    grad_proj = (grad_proj * recip).astype(BF)
    coef = jnp.sum(grad_proj.astype(F32) * raw, axis=-1) * (recip[:, 0] * recip[:, 0]) / model
    coef = jnp.broadcast_to(coef[None], (8, seq))
    grad_proj_next, mixed_next, coef = exchange("dp", [grad_proj, mixed, coef], [False] * 3, 5)
    grad_proj_next = grad_proj_next.reshape(rows, cols)
    coef = coef[:, 0].reshape(rows, 1)
    back = dot(grad_proj_next, qkv, 1, 1) * gain - carried.astype(F32) * coef
    returned = relay(back.astype(BF), held, 6)

    part = dot(returned, out, 1, 0).astype(BF).reshape(count, seq, head_cols)
    (part,) = exchange("dp", [part], [True], 7)
    grad_proj = attend_back(query, key, value, probs, summed(part).astype(BF), seq, groups)
    grad_proj = (grad_proj * recip).astype(BF)
    (grad_proj,) = exchange("dp", [grad_proj], [False], 8)

    block_in = jnp.where(first, held, carried)
    grad_out = jnp.where(first, returned, held)
    mixed_all = jnp.where(first, mixed_start, mixed_next.reshape(rows, head_cols))
    grad_proj = jnp.where(first, grad_proj.reshape(rows, cols), grad_proj_next)
    out_grad = dot(grad_out, mixed_all, 0, 0)
    weight = dot(block_in, grad_proj, 0, 0)
    qkv_grad = weight * gain.reshape(width, 1)
    gain_grad = lax.psum(jnp.sum(weight * qkv.astype(F32), axis=-1), "tensor")
    return qkv_grad[None], out_grad[None], gain_grad[None]


def solution(mesh):
    in_specs = (
        P("dp", None, None),
        P("pipe", None),
        P("pipe", "dp", "tensor"),
        P("pipe", "dp", "tensor"),
        P("dp", None, None),
    )
    out_specs = (P("pipe", "dp", "tensor"), P("pipe", "dp", "tensor"), P("pipe", "dp"))
    return jax.shard_map(shards, mesh=mesh, in_specs=in_specs, out_specs=out_specs, check_vma=False)
```

time: 1440 us -> 425 us (0.30)
  waiting for transfers between devices: 1100 us -> 0 us
  Pallas kernels: 0 us -> 302 us
  matrix products: 197 us -> 49.1 us
  other arithmetic: 75 us -> 17.8 us
  starting transfers between devices: 22.4 us -> 0 us
  local copies, waits for them, and re-layouts: 26 us -> 44.5 us
    all_gather x2 -> x0, waiting for transfers between devices: 367 us -> none  [the longest x1 218 us: shards(): lax.all_gather(qkv_weight, 'dp', axis=1, tiled=True)]
    reduce_scatter x2 -> x0, waiting for transfers between devices: 357 us -> none  [the longest x1 211 us: shards(): lax.psum_scatter(weight_part[None].astype(jnp.bfloat16), 'dp', scatter_di...]
    psum x10 -> x0, waiting for transfers between devices: 327 us -> none  [heads_total(): lax.psum(partial_rows.astype(jnp.bfloat16), 'tensor').astype(jnp.float32)]
    pallas_call x0 -> x9, Pallas kernels: none -> 302 us  [the longest x7 240 us: exchange(): pl.pallas_call(functools.partial(exchange_kernel, axis, spread, count), o...]
    dot_general x52 -> x19, matrix products: 188 us -> 45.7 us  [the longest x8 23.2 us: dot(): lax.dot_general(a, b, (((ca,), (cb,)), ((), ())), preferred_element_type=...]
    select_n x50 -> x1, other arithmetic: 47.9 us -> 1.08 us  [shards(): held = jnp.where(first, tokens[0], cotangent[0])]
    ppermute x10 -> x0, waiting for transfers between devices: 34.2 us -> none  [from_behind(): lax.ppermute(value, axis, [(source, source + steps) for source in range(l...]
    ppermute x10 -> x0, starting transfers between devices: 21.9 us -> none  [from_behind(): lax.ppermute(value, axis, [(source, source + steps) for source in range(l...]
  transfers between devices with their start and end apart: 25 -> 0, of which waited for: 25 -> 0; matrix products, arithmetic and copies ran while one was open for 3% -> 0% of each run, Pallas kernels for 0% -> 0%
where the time goes in v1:
time: 425 us; the launch traced here: 421 us
  Pallas kernels  302 us (71%)
  matrix products  49.1 us (12%)
  local copies, waits for them, and re-layouts  44.5 us (10%)
  other arithmetic  17.8 us (4%)
  blocking collectives  6.02 us (1%)
    pallas_call x7, Pallas kernels, exchange(): pl.pallas_call(functools.partial(exchange_kernel, axis, spread, count), o...  240 us
    pallas_call x2, Pallas kernels, relay(): pl.pallas_call(functools.partial(relay_kernel, count), out_shape=jax.Shap...  62.3 us
    dot_general x8, matrix products, dot(): lax.dot_general(a, b, (((ca,), (cb,)), ((), ())), preferred_element_type=...  23.2 us
    unnamed x51, local copies, waits for them, and re-layouts  11.4 us
    reduce_sum x5, local copies, waits for them, and re-layouts, summed(): return jnp.sum(slots.astype(F32), axis=0)  9.99 us

profile of v1, /device:TPU:25, one launch (start us, length us, event | category | flops | bytes accessed | tf_op | source)
XLA Modules:
  0.0 420.9 jit_solution(8553931864119390579)
XLA Ops:
  1.5 1.6 copy.99
  3.1 2.3 copy.100
  5.4 1.1 broadcast_select_fusion
  6.5 2.3 copy.101
  8.7 1.2 copy-done.9
  9.9 25.0 %shard_map.76 = bf16[4,128,1024]{2,1,0:T(8,128)(2,1)S(1)} custom-call(bf16[4,128,1024]{2,1,0:T(8,128)(2,1)S(1)} %bitcast.176), custom_call_target="tpu_custom_call" | custom-call | tf_op jit(solution)/shard_map/pallas_call | solution.py:67
  35.4 1.3 fusion.36
  37.2 1.8 fusion.18
  39.1 35.8 %shard_map.77 = (bf16[4,128,1536]{2,1,0:T(8,128)(2,1)S(1)}, f32[4,8,128]{2,1,0:T(8,128)S(1)}) custom-call(bf16[4,128,1536]{2,1,0:T(8,128)(2,1)S(1)} %bitcast.177, f32[4,8,128]{2,1,0:T(8,128)S(1)} %broadcast_in_dim.71.refs_1_), custom_call_target="tpu_custom_call" | custom-call | tf_op jit(solution)/shard_map/pallas_call | solution.py:67
  75.1 0.9 copy-done.18
  76.7 1.1 copy.111
  77.9 0.8 copy.112
  78.7 2.3 copy.102
  81.0 2.3 copy.103
  83.3 1.3 fusion.74
  86.0 1.3 fusion.104
  87.3 2.0 fusion.56
  89.3 2.4 convolution_convert_fusion.1
  91.7 1.9 copy.163
  93.6 1.1 reshape.208.refs_0_
  94.7 22.9 %shard_map.78 = bf16[4,128,1024]{2,1,0:T(8,128)(2,1)S(1)} custom-call(bf16[128,1024]{1,0:T(8,128)(2,1)S(1)} %reshape.208.refs_0_), custom_call_target="tpu_custom_call" | custom-call | tf_op jit(solution)/shard_map/pallas_call | solution.py:67
  117.7 2.3 fusion.39
  120.0 1.2 copy-done.14
  121.2 33.7 %shard_map.79 = bf16[4,128,1024]{2,1,0:T(8,128)(2,1)S(1)} custom-call(bf16[4,128,1024]{2,1,0:T(8,128)(2,1)S(1)} %bitcast.179, bf16[128,1024]{1,0:T(8,128)(2,1)S(1)} %dynamic-slice_bitcast_fusion.rest_ref), custom_call_target="tpu_custom_call" | custom-call | tf_op jit(solution)/shard_map/pallas_call | solution.py:151
  155.3 1.8 fusion.15
  157.1 35.9 %shard_map.80 = (bf16[4,128,1536]{2,1,0:T(8,128)(2,1)S(1)}, f32[4,8,128]{2,1,0:T(8,128)S(1)}) custom-call(bf16[4,128,1536]{2,1,0:T(8,128)(2,1)S(1)} %bitcast.178, f32[4,8,128]{2,1,0:T(8,128)S(1)} %broadcast_in_dim.73.refs_1_), custom_call_target="tpu_custom_call" | custom-call | tf_op jit(solution)/shard_map/pallas_call | solution.py:67
  193.1 1.1 copy-done.10
  194.2 2.6 convert_reduce_fusion
  196.8 2.3 copy.107
  199.1 2.3 copy.109
  201.4 1.3 fusion.75
  204.2 2.1 fusion.105
  206.3 1.4 convolution_bitcast_fusion.3
  207.7 1.9 fusion.81
  209.5 2.7 convolution_bitcast_fusion.4
  212.2 2.9 fusion.64
  215.1 2.0 maximum_bitcast_fusion
  217.1 2.3 copy.121
  219.4 2.3 copy.122
  221.7 2.0 multiply_convert_fusion.3.refs_0_
  223.7 1.3 convolution_convert_fusion
  225.1 0.9 copy.162
  226.0 1.8 reshape.218.refs_1_
  227.8 1.7 multiply_reduce_fusion.3
  229.5 59.6 %shard_map.81 = (bf16[4,128,1536]{2,1,0:T(8,128)(2,1)S(1)}, bf16[4,128,1024]{2,1,0:T(8,128)(2,1)S(1)}, f32[4,8,128]{2,1,0:T(8,128)S(1)}) custom-call(bf16[128,1536]{1,0:T(8,128)(2,1)S(1)} %copy-done.11, bf16[128,1024]{1,0:T(8,128)(2,1)S(1)} %copy-done.15, f32[8,128]{1,0:T(8,128)S(1)} %broadcast_in_dim.77.refs_2_), custom_call_target="tpu_custom_call" | custom-call | tf_op jit(solution)/shard_map/pallas_call | solution.py:67
  289.1 4.6 %fusion.24 = bf16[512,1024]{1,0:T(8,128)(2,1)S(1)} fusion(bf16[512,1536]{1,0:T(8,128)(2,1)S(1)} %bitcast.182, bf16[1,1024,1536]{2,1,0:T(8,128)(2,1)} %param.7, f32[512]{0:T(512)S(1)} %bitcast.220, f32[1024]{0:T(1024)S(1)} %bitcast.213, bf16[4,128,1024]{2,1,0:T(8,128)(2,1)S(1)} %copy-done.6), kind=kOutput, calls=%fused_computation.26 | convolution fusion | flops 1613234176 | bytes 6821888 | tf_op jit(solution)/shard_map/dot_general | solution.py:20
  293.8 28.6 %shard_map.82 = bf16[4,128,1024]{2,1,0:T(8,128)(2,1)S(1)} custom-call(bf16[4,128,1024]{2,1,0:T(8,128)(2,1)S(1)} %bitcast.180, bf16[128,1024]{1,0:T(8,128)(2,1)S(1)} %dynamic-slice_bitcast_fusion.rest_ref), custom_call_target="tpu_custom_call" | custom-call | tf_op jit(solution)/shard_map/pallas_call | solution.py:151
  322.4 1.3 fusion.42
  323.7 24.3 %shard_map.83 = bf16[4,128,1024]{2,1,0:T(8,128)(2,1)S(1)} custom-call(bf16[4,128,1024]{2,1,0:T(8,128)(2,1)S(1)} %bitcast.181), custom_call_target="tpu_custom_call" | custom-call | tf_op jit(solution)/shard_map/pallas_call | solution.py:67
  347.9 1.0 copy-done.8
  348.9 1.4 reduce_sum.139
  351.2 1.1 copy.126
  352.3 1.3 convolution_bitcast_fusion.1
  353.6 1.9 fusion.80
  355.5 2.0 convolution_bitcast_fusion.2
  357.5 2.8 fusion.69
  360.3 2.0 copy.132
  362.4 2.0 pad_maximum_fusion
  364.4 2.3 copy.135
  366.7 1.4 multiply_convert_fusion.1.refs_0_
  368.1 36.6 %shard_map.84 = bf16[4,128,1536]{2,1,0:T(8,128)(2,1)S(1)} custom-call(bf16[128,1536]{1,0:T(8,128)(2,1)S(1)} %multiply_convert_fusion.1.refs_0_), custom_call_target="tpu_custom_call" | custom-call | tf_op jit(solution)/shard_map/pallas_call | solution.py:67
  404.7 6.8 %fusion.5 = (f32[1024]{0:T(1024)S(1)}, f32[1,1024,1536]{2,1,0:T(8,128)}) fusion(bf16[1,1024,1536]{2,1,0:T(8,128)(2,1)} %param.7, f32[1024]{0:T(1024)S(1)} %bitcast.214, bf16[4,128,1536]{2,1,0:T(8,128)(2,1)S(1)} %shard_map.84, bf16[4,128,1536]{2,1,0:T(8,128)(2,1)S(1)} %copy-done.17, pred[]{:T(512)S(6)} %eq.3, bf16[4,128,1024]{2,1,0:T(8,128)(2,1)S(1)} %shard_map.76, ...), kind=kOutput, calls=%fused_computation.7 | convolution fusion | flops 1618213888 | bytes 14688257 | tf_op jit(solution)/shard_map/dot_general | solution.py:20
  411.6 3.3 convolution_bitcast_fusion
  414.9 6.0 %psum.7 = f32[1,1024]{1,0:T(1,128)} all-reduce(f32[1,1024]{1,0:T(1,128)S(1)} %bitcast.219), channel_id=1, replica_groups=mesh['pipe'=2,'tensor'=4,'dp'=4] {'tensor'}, use_global_device_ids=true, to_apply=%region_15.16 | all-reduce | flops 1024 | bytes 8192 | tf_op jit(solution)/shard_map/psum | solution.py:271
  (66 shorter events, 7.1 us)
Async XLA Ops:
  0.6 34.7 %copy-start = (bf16[1,1024,1024]{2,1,0:T(8,128)(2,1)S(1)}, bf16[1,1024,1024]{2,1,0:T(8,128)(2,1)}, u32[]{:S(2)}) copy-start(bf16[1,1024,1024]{2,1,0:T(8,128)(2,1)} %param.8) | copy-start | bytes 6291460
  8.7 1.2 copy-start.9
  35.3 1.9 copy-start.22
  75.1 0.9 copy-start.18
  117.6 2.3 copy-start.3
  119.9 1.2 copy-start.14
  121.2 34.1 %copy-start.23 = (bf16[1,1024,1536]{2,1,0:T(8,128)(2,1)S(1)}, bf16[1,1024,1536]{2,1,0:T(8,128)(2,1)}, u32[]{:S(2)}) copy-start(bf16[1,1024,1536]{2,1,0:T(8,128)(2,1)} %param.7) | copy-start | bytes 9437188
  154.9 2.2 copy-start.5
  193.1 1.1 copy-start.10
  199.1 5.1 %copy-start.21 = (pred[16,8,4,128]{3,1,2,0:T(8,128)(4,1)S(1)}, pred[16,8,4,128]{3,1,2,0:T(8,128)(4,1)}, u32[]{:S(2)}) copy-start(pred[16,8,4,128]{3,1,2,0:T(8,128)(4,1)} %copy.164) | copy-start | bytes 196612
  202.7 0.7 copy-start.19
  206.3 1.4 copy-start.20
  227.8 1.7 copy-start.11
  227.8 1.7 copy-start.15
  227.8 61.3 %copy-start.6 = (bf16[4,128,1024]{2,1,0:T(8,128)(2,1)S(1)}, bf16[4,128,1024]{2,1,0:T(8,128)(2,1)}, u32[]{:S(2)}) copy-start(bf16[4,128,1024]{2,1,0:T(8,128)(2,1)} %copy-done.5) | copy-start | bytes 3145732
  289.1 4.7 %copy-start.12 = (bf16[4,128,1024]{2,1,0:T(8,128)(2,1)}, bf16[4,128,1024]{2,1,0:T(8,128)(2,1)S(1)}, u32[]{:S(2)}) copy-start(bf16[4,128,1024]{2,1,0:T(8,128)(2,1)S(1)} %get-tuple-element.16) | copy-start | bytes 3145732
  289.1 4.7 %copy-start.16 = (bf16[4,128,1536]{2,1,0:T(8,128)(2,1)}, bf16[4,128,1536]{2,1,0:T(8,128)(2,1)S(1)}, u32[]{:S(2)}) copy-start(bf16[4,128,1536]{2,1,0:T(8,128)(2,1)S(1)} %get-tuple-element.14) | copy-start | bytes 4718596
  322.4 1.3 copy-start.1
  347.9 1.0 copy-start.8
  366.7 38.0 %copy-start.7 = (bf16[4,128,1024]{2,1,0:T(8,128)(2,1)S(1)}, bf16[4,128,1024]{2,1,0:T(8,128)(2,1)}, u32[]{:S(2)}) copy-start(bf16[4,128,1024]{2,1,0:T(8,128)(2,1)} %copy-done.5) | copy-start | bytes 3145732
  366.7 38.0 %copy-start.17 = (bf16[4,128,1536]{2,1,0:T(8,128)(2,1)S(1)}, bf16[4,128,1536]{2,1,0:T(8,128)(2,1)}, u32[]{:S(2)}) copy-start(bf16[4,128,1536]{2,1,0:T(8,128)(2,1)} %copy-done.16) | copy-start | bytes 4718596
  404.7 6.9 %copy-start.2 = (bf16[4,128,1024]{2,1,0:T(8,128)(2,1)S(1)}, bf16[4,128,1024]{2,1,0:T(8,128)(2,1)}, u32[]{:S(2)}) copy-start(bf16[4,128,1024]{2,1,0:T(8,128)(2,1)} %copy-done.1) | copy-start | bytes 3145732
  404.7 6.9 %copy-start.4 = (bf16[4,128,1024]{2,1,0:T(8,128)(2,1)S(1)}, bf16[4,128,1024]{2,1,0:T(8,128)(2,1)}, u32[]{:S(2)}) copy-start(bf16[4,128,1024]{2,1,0:T(8,128)(2,1)} %copy-done.3) | copy-start | bytes 3145732
  404.7 6.9 %copy-start.13 = (bf16[4,128,1024]{2,1,0:T(8,128)(2,1)S(1)}, bf16[4,128,1024]{2,1,0:T(8,128)(2,1)}, u32[]{:S(2)}) copy-start(bf16[4,128,1024]{2,1,0:T(8,128)(2,1)} %copy-done.12) | copy-start | bytes 3145732

commit v2 on v1

v2 whole, which is shorter than its diff:
```python
import functools

import jax
import jax.numpy as jnp
from jax import lax
from jax.experimental import pallas as pl
from jax.experimental.pallas import tpu as pltpu
from jax.sharding import PartitionSpec as P

HD = 128
GROUP = 4
EPSILON = 1e-05
BF = jnp.bfloat16
F32 = jnp.float32
MESH = pl.DeviceIdType.MESH


def dot(a, b, ca, cb):
    return lax.dot_general(a, b, (((ca,), (cb,)), ((), ())), preferred_element_type=F32)


def meet(peers):
    barrier = pltpu.get_barrier_semaphore()
    for peer in peers:
        pl.semaphore_signal(barrier, inc=1, device_id=peer, device_id_type=MESH)
    pl.semaphore_wait(barrier, len(peers))


def others(axis):
    me, count = lax.axis_index(axis), lax.axis_size(axis)
    return [lax.rem(me + step, count) for step in range(1, count)]


def push(src, dst, sems, place, peer):
    copy = pltpu.make_async_remote_copy(
        src_ref=src,
        dst_ref=dst,
        send_sem=sems.at[(0, *place)],
        recv_sem=sems.at[(1, *place)],
        device_id=peer,
        device_id_type=MESH,
    )
    copy.start()
    return copy


def beside():
    tensor = lax.axis_index("tensor")
    core, chip = lax.rem(tensor, 2), tensor // 2
    return tensor, core, chip, chip * 2 + 1 - core, (1 - chip) * 2 + core


def call(kernel, collective_id, arrays, outs, scratch):
    vmem = pl.BlockSpec(memory_space=pltpu.VMEM)
    return pl.pallas_call(
        kernel,
        out_shape=[jax.ShapeDtypeStruct(shape, dtype) for shape, dtype in outs],
        in_specs=[vmem] * len(arrays),
        out_specs=[vmem] * len(outs),
        scratch_shapes=scratch,
        compiler_params=pltpu.CompilerParams(
            collective_id=collective_id, has_side_effects=True, vmem_limit_bytes=48 << 20
        ),
    )(*arrays)


def spread_kernel(count, tokens_ref, cotangent_ref, out_ref, picked, dp_sems, chip_sems, core_sems, far_sems):
    me = lax.axis_index("dp")
    tensor, core, chip, sibling, across = beside()
    peers = others("dp")
    meet([{"dp": p} for p in peers] + [{"tensor": sibling}, {"tensor": across}])
    rows, width = picked.shape[0], out_ref.shape[2]
    mine = pl.ds(pl.multiple_of(tensor * rows, rows), rows)
    far = pl.ds(pl.multiple_of(across * rows, rows), rows)
    first = lax.axis_index("pipe") == 0
    picked[...] = jnp.where(first, tokens_ref[mine, :], cotangent_ref[mine, :])
    copies, later = [], []
    for step, peer in enumerate(peers, 1):
        block = picked.at[:, pl.ds(pl.multiple_of(peer * width, width), width)]
        copies.append(push(block, out_ref.at[me, mine], dp_sems, (step,), {"dp": peer}))
    out_ref[me, mine, :] = picked[:, pl.ds(pl.multiple_of(me * width, width), width)]
    for step in range(count):
        source = lax.rem(me + count - step, count)
        if step:
            copies[step - 1].wait_recv()
        block = out_ref.at[source, mine]
        later.append(push(block, block, chip_sems, (step,), {"tensor": across}))
        copies.append(push(block, block, core_sems, (step,), {"tensor": sibling}))
    for step in range(count):
        source = lax.rem(me + count - step, count)
        later[step].wait_recv()
        block = out_ref.at[source, far]
        copies.append(push(block, block, far_sems, (step,), {"tensor": sibling}))
    for step, copy in enumerate(copies):
        if step >= count - 1:
            copy.wait_recv()
        copy.wait_send()
    for copy in later:
        copy.wait_send()


def spread(tokens, cotangent, width, collective_id):
    count = lax.axis_size("dp")
    seq, model = tokens.shape
    dma = pltpu.SemaphoreType.DMA((2, count))
    (out,) = call(
        functools.partial(spread_kernel, count),
        collective_id,
        [tokens, cotangent],
        [((count, seq, width), BF)],
        [pltpu.VMEM((seq // lax.axis_size("tensor"), model), BF), dma, dma, dma, dma],
    )
    return out


def relay_kernel(chunks, beside_z, *refs):
    if beside_z:
        part_ref, rest_ref, extra_ref, out_ref, gathered = refs[:5]
        near, half, landed, own, core_sems, sems, dp_sems = refs[5:]
    else:
        part_ref, rest_ref, out_ref, near, half, landed, own, core_sems, sems = refs
    tensor, core, chip, sibling, across = beside()
    section = {"pipe": 1 - lax.axis_index("pipe")}
    me = lax.axis_index("dp")
    peers = others("dp") if beside_z else []
    meet([{"dp": p} for p in peers] + [{"tensor": sibling}, {"tensor": across}, section])
    sibling_to, across_to = {"tensor": sibling}, {"tensor": across}
    rows = own.shape[0] // chunks
    cut = [pl.ds(k * rows, rows) for k in range(chunks)]
    held, firsts, seconds, across_x, fans, ends = [], [], [], [], [], []
    for k in range(chunks):
        give = (1 - chip) * 2 + 1 - core
        firsts.append(push(part_ref.at[give, cut[k]], near.at[0, cut[k]], core_sems, (0, k), sibling_to))
    for k in range(chunks):
        held.append(push(part_ref.at[sibling, cut[k]], near.at[1, cut[k]], core_sems, (1, k), sibling_to))
    for step, peer in enumerate(peers, 1):
        seconds.append(push(extra_ref, gathered.at[me], dp_sems, (step,), {"dp": peer}))
    if beside_z:
        gathered[me] = extra_ref[...]
    outs = []
    for k in range(chunks):
        firsts[k].wait_recv()
        half[cut[k], :] = (part_ref[across, cut[k], :].astype(F32) + near[0, cut[k], :].astype(F32)).astype(BF)
        outs.append(push(half.at[cut[k]], landed.at[cut[k]], sems, (0, k), across_to))
    for k in range(chunks):
        held[k].wait_recv()
        total = rest_ref[cut[k], :].astype(F32) + part_ref[tensor, cut[k], :].astype(F32)
        total = total + near[1, cut[k], :].astype(F32)
        outs[k].wait_recv()
        own[cut[k], :] = (total + landed[cut[k], :].astype(F32)).astype(BF)
        across_x.append(push(own.at[cut[k]], out_ref.at[tensor, cut[k]], sems, (1, k), section))
    for k in range(chunks):
        across_x[k].wait_recv()
        block = out_ref.at[tensor, cut[k]]
        fans.append(push(block, block, sems, (2, k), across_to))
        ends.append(push(block, block, core_sems, (2, k), sibling_to))
    for k in range(chunks):
        fans[k].wait_recv()
        block = out_ref.at[across, cut[k]]
        ends.append(push(block, block, core_sems, (3, k), sibling_to))
    for copy in ends + seconds:
        copy.wait_recv()
    for copy in firsts + held + outs + across_x + fans + ends + seconds:
        copy.wait_send()


def relay(parts, rest, collective_id, extra=None):
    count, dp = lax.axis_size("tensor"), lax.axis_size("dp")
    rows, width = parts.shape[0] // count, parts.shape[1]
    chunks = 4
    parts = parts.reshape(count, rows, width)
    own = lax.dynamic_index_in_dim(rest.reshape(count, rows, width), lax.axis_index("tensor"), 0, False)
    more = [] if extra is None else [extra]
    block = pltpu.VMEM((rows, width), BF)
    results = call(
        functools.partial(relay_kernel, chunks, bool(more)),
        collective_id,
        [parts, own] + more,
        [(parts.shape, BF)] + [((dp, *a.shape), a.dtype) for a in more],
        [
            pltpu.VMEM((2, rows, width), BF),
            block,
            block,
            block,
            pltpu.SemaphoreType.DMA((2, 4, chunks)),
            pltpu.SemaphoreType.DMA((2, 3, chunks)),
        ]
        + [pltpu.SemaphoreType.DMA((2, dp)) for a in more],
    )
    out = results[0].reshape(count * rows, width)
    return (out, results[1]) if more else out


def column(row):
    size = row.shape[1]
    same = lax.broadcasted_iota(jnp.int32, (size, size), 0) == lax.broadcasted_iota(jnp.int32, (size, size), 1)
    return jnp.sum(jnp.where(same, row, 0.0), axis=1, keepdims=True)


def as_row(col):
    size = col.shape[0]
    same = lax.broadcasted_iota(jnp.int32, (size, size), 0) == lax.broadcasted_iota(jnp.int32, (size, size), 1)
    return jnp.sum(jnp.where(same, col, 0.0), axis=0, keepdims=True)


def head(index):
    return pl.ds(index * HD, HD)


def probs_of(query, key):
    seq = query.shape[0]
    scores = dot(query, key, 1, 1) * HD**-0.5
    allowed = lax.broadcasted_iota(jnp.int32, (seq, seq), 1) <= lax.broadcasted_iota(jnp.int32, (seq, seq), 0)
    scores = jnp.where(allowed, scores, -jnp.inf)
    raised = jnp.exp(scores - jnp.max(scores, axis=-1, keepdims=True))
    return raised / jnp.sum(raised, axis=-1, keepdims=True)


def stage_kernel(mode, count, model, *refs):
    if mode == "forward":
        part, stat, raw_out, proj, stat_out, result, landed, stats, scatter, gather, small = refs
    elif mode == "both":
        part, stat, grads, result, coef_out, mixed_out, landed, stats, proj, scatter, gather, small = refs
    else:
        part, proj, stat, result, landed, probs_all, scatter, gather = refs
    me = lax.axis_index("dp")
    peers = others("dp")
    meet([{"dp": p} for p in peers])
    groups = scatter.shape[1]
    seq = part.shape[1]
    cols = part.shape[2] // groups
    full = (GROUP + 2) * HD
    low = GROUP * HD
    copies, arrivals, ends, stat_copies = [], [], [], []
    if mode != "backward":
        for step, peer in enumerate(peers, 1):
            stat_copies.append(push(stat.at[peer], stats.at[step], small, (0, step), {"dp": peer}))
    for g in range(groups):
        strip = pl.ds(g * cols, cols)
        arrivals.append(
            [
                push(part.at[peer, :, strip], landed.at[step, :, strip], scatter, (g, step), {"dp": peer})
                for step, peer in enumerate(peers, 1)
            ]
        )
    if mode == "backward":
        recip = lax.rsqrt(column(stat[0:1, :]) / model + EPSILON)
        for g in range(groups):
            for j in range(GROUP):
                query, key = proj[:, head(g * (GROUP + 2) + j)], proj[:, head(g * (GROUP + 2) + GROUP)]
                probs_all[g * GROUP + j] = probs_of(query, key)
    else:
        squares = stat[me]
        for step, copy in enumerate(stat_copies, 1):
            copy.wait_recv()
            squares = squares + stats[step]
        recip = lax.rsqrt(column(squares[0:1, :]) / model + EPSILON)
        if mode == "forward":
            stat_out[...] = squares
    coef = jnp.zeros((seq, 1), F32)
    for g in range(groups):
        base = g * full
        for copy in arrivals[g]:
            copy.wait_recv()

        def total(at):
            sums = part[me, :, at].astype(F32)
            for step in range(1, count):
                sums = sums + landed[step, :, at].astype(F32)
            return sums

        if mode != "backward":
            for i in range(GROUP + 2):
                at = pl.ds(base + i * HD, HD)
                raw = total(at)
                if mode == "forward":
                    raw_out[:, at] = raw.astype(BF)
                proj[:, at] = (raw * recip).astype(BF)
        key, value = proj[:, pl.ds(base + low, HD)], proj[:, pl.ds(base + low + HD, HD)]
        grad_key = jnp.zeros((seq, HD), F32)
        grad_value = jnp.zeros((seq, HD), F32)
        for j in range(GROUP):
            at = pl.ds(base + j * HD, HD)
            mixed_at = pl.ds(g * low + j * HD, HD)
            query = proj[:, at]
            probs = probs_all[g * GROUP + j] if mode == "backward" else probs_of(query, key)
            probs_low = probs.astype(BF)
            if mode != "backward":
                mixed = dot(probs_low, value, 1, 0).astype(BF)
            if mode == "forward":
                result[me, :, mixed_at] = mixed
                continue
            if mode == "both":
                mixed_out[:, mixed_at] = mixed
                grad = grads[:, mixed_at]
            else:
                grad = total(mixed_at).astype(BF)
            grad_low = dot(grad, value, 1, 1)
            inner = jnp.sum(probs * grad_low, axis=-1, keepdims=True)
            grad_score = (probs * (grad_low - inner) * HD**-0.5).astype(BF)
            grad_query = dot(grad_score, key, 1, 0)
            grad_key = grad_key + dot(grad_score, query, 0, 0)
            grad_value = grad_value + dot(probs_low, grad, 0, 0)
            result[me, :, at] = (grad_query * recip).astype(BF)
            if mode == "both":
                coef = coef + jnp.sum(grad_query * query.astype(F32), axis=-1, keepdims=True)
        if mode == "forward":
            strip = pl.ds(g * low, low)
        else:
            strip = pl.ds(base, full)
            result[me, :, pl.ds(base + low, HD)] = (grad_key * recip).astype(BF)
            result[me, :, pl.ds(base + low + HD, HD)] = (grad_value * recip).astype(BF)
            if mode == "both":
                coef = coef + jnp.sum(grad_key * key.astype(F32), axis=-1, keepdims=True)
                coef = coef + jnp.sum(grad_value * value.astype(F32), axis=-1, keepdims=True)
        for step, peer in enumerate(peers, 1):
            block = result.at[me, :, strip]
            ends.append(push(block, block, gather, (g, step), {"dp": peer}))
    if mode == "both":
        coef_out[me] = jnp.broadcast_to(as_row(coef * recip * recip / model), coef_out.shape[1:])
        for step, peer in enumerate(peers, 1):
            block = coef_out.at[me]
            ends.append(push(block, block, small, (1, step), {"dp": peer}))
    for copy in ends:
        copy.wait()
    for copy in sum(arrivals, stat_copies):
        copy.wait_send()


def stage(mode, arrays, groups, model, collective_id):
    part = arrays[0]
    count, seq, cols = part.shape
    full = groups * (GROUP + 2) * HD
    low = groups * GROUP * HD
    dma = pltpu.SemaphoreType.DMA
    sems = [dma((2, groups, count)), dma((2, groups, count))]
    landed = pltpu.VMEM(part.shape, BF)
    if mode == "backward":
        outs = [((count, seq, full), BF)]
        scratch = [landed, pltpu.VMEM((groups * GROUP, seq, seq), F32), *sems]
    else:
        stats = pltpu.VMEM((count, 8, seq), F32)
        if mode == "forward":
            outs = [((seq, full), BF), ((seq, full), BF), ((8, seq), F32), ((count, seq, low), BF)]
            scratch = [landed, stats, *sems, dma((2, 2, count))]
        else:
            outs = [((count, seq, full), BF), ((count, 8, seq), F32), ((seq, low), BF)]
            scratch = [landed, stats, pltpu.VMEM((seq, full), BF), *sems, dma((2, 2, count))]
    return call(functools.partial(stage_kernel, mode, count, model), collective_id, arrays, outs, scratch)


def total_kernel(count, in_ref, out_ref, landed, sems):
    meet([{"tensor": p} for p in others("tensor")])
    copies = [
        push(in_ref, landed.at[step], sems, (step,), {"tensor": peer})
        for step, peer in enumerate(others("tensor"), 1)
    ]
    total = in_ref[...]
    for step, copy in enumerate(copies, 1):
        copy.wait_recv()
        total = total + landed[step]
    out_ref[...] = total
    for copy in copies:
        copy.wait_send()


def tensor_total(array, collective_id):
    count = lax.axis_size("tensor")
    scratch = [pltpu.VMEM((count, *array.shape), F32), pltpu.SemaphoreType.DMA((2, count))]
    return call(functools.partial(total_kernel, count), collective_id, [array], [(array.shape, F32)], scratch)[0]


def shards(tokens, norm_gains, qkv_weight, out_weight, cotangent):
    first = lax.axis_index("pipe") == 0
    count = lax.axis_size("dp")
    qkv, out = qkv_weight[0], out_weight[0]
    width, cols = qkv.shape
    head_cols = out.shape[1]
    seq, model = tokens.shape[1:]
    rows = count * seq
    groups = cols // ((GROUP + 2) * HD)
    gain = lax.dynamic_slice_in_dim(norm_gains[0], lax.axis_index("dp") * width, width, 0)[None]

    def project(block):
        scaled = block.astype(F32)
        squares = jnp.sum(scaled * scaled, axis=-1).reshape(count, 1, seq)
        squares = jnp.broadcast_to(squares, (count, 8, seq))
        return dot((scaled * gain).astype(BF), qkv, 1, 0).astype(BF), squares

    held = spread(tokens[0], cotangent[0], width, 0).reshape(rows, width)

    proj_part, squares = project(held)
    mixed_part = jnp.pad(dot(held, out, 1, 0).astype(BF), ((0, 0), (0, cols - head_cols)))
    part = jnp.where(first, proj_part, mixed_part).reshape(count, seq, cols)
    grads, proj, squares, mixed_start = stage("forward", [part, squares], groups, model, 1)
    mixed_start = mixed_start.reshape(rows, head_cols)
    carried = relay(dot(mixed_start, out, 1, 1).astype(BF), held, 2)

    part, next_squares = project(carried)
    part = part.reshape(count, seq, cols)
    grad_proj_next, coef, mixed = stage("both", [part, next_squares, grads], groups, model, 3)
    grad_proj_next = grad_proj_next.reshape(rows, cols)
    coef = coef[:, 0].reshape(rows, 1)
    back = dot(grad_proj_next, qkv, 1, 1) * gain - carried.astype(F32) * coef
    returned, mixed_next = relay(back.astype(BF), held, 4, mixed)

    part = dot(returned, out, 1, 0).astype(BF).reshape(count, seq, head_cols)
    (grad_proj,) = stage("backward", [part, proj, squares], groups, model, 5)

    block_in = jnp.where(first, held, carried)
    grad_out = jnp.where(first, returned, held)
    mixed_all = jnp.where(first, mixed_start, mixed_next.reshape(rows, head_cols))
    grad_proj = jnp.where(first, grad_proj.reshape(rows, cols), grad_proj_next)
    out_grad = dot(grad_out, mixed_all, 0, 0)
    weight = dot(block_in, grad_proj, 0, 0)
    qkv_grad = weight * gain.reshape(width, 1)
    gain_part = jnp.sum(weight * qkv.astype(F32), axis=-1)
    gain_grad = tensor_total(gain_part.reshape(width // 128, 128), 6).reshape(1, width)
    return qkv_grad[None], out_grad[None], gain_grad


def solution(mesh):
    in_specs = (
        P("dp", None, None),
        P("pipe", None),
        P("pipe", "dp", "tensor"),
        P("pipe", "dp", "tensor"),
        P("dp", None, None),
    )
    out_specs = (P("pipe", "dp", "tensor"), P("pipe", "dp", "tensor"), P("pipe", "dp"))
    return jax.shard_map(shards, mesh=mesh, in_specs=in_specs, out_specs=out_specs, check_vma=False)
```

time: 425 us -> 286 us (0.67)
  Pallas kernels: 302 us -> 256 us
  local copies, waits for them, and re-layouts: 44.5 us -> 5.16 us
  matrix products: 49.1 us -> 22.2 us
  other arithmetic: 17.8 us -> 1.65 us
  blocking collectives: 6.02 us -> 0 us
    pallas_call x9 -> x7, Pallas kernels: 302 us -> 256 us  [call(): pl.pallas_call(kernel, out_shape=[jax.ShapeDtypeStruct(shape, dtype) for...]
    dot_general x11 -> x0, matrix products: 22.5 us -> none  [the longest x2 5.66 us: attend_back(): jnp.einsum('grc,gcd->grd', grad_score, key, preferred_element_type=F32)]
    reshape x7 -> x0, local copies, waits for them, and re-layouts: 12.3 us -> none  [the longest x2 4.58 us: attend_back(): jnp.transpose(heads, (2, 0, 1, 3)).reshape(seq, groups * (GROUP + 2) * HD)]
    reduce_sum x5 -> x0, local copies, waits for them, and re-layouts: 9.99 us -> none  [summed(): return jnp.sum(slots.astype(F32), axis=0)]
    unnamed x51 -> x19, local copies, waits for them, and re-layouts: 11.4 us -> 4.3 us
    psum x1 -> x0, blocking collectives: 6.02 us -> none  [shards(): gain_grad = lax.psum(jnp.sum(weight * qkv.astype(F32), axis=-1), 'tensor')]
    reduce_sum x6 -> x0, other arithmetic: 5.94 us -> none  [the longest x5 4.25 us: summed(): return jnp.sum(slots.astype(F32), axis=0)]
    transpose x3 -> x0, other arithmetic: 4.62 us -> none  [the longest x2 2.57 us: split_heads(): return jnp.transpose(flat.reshape(seq, groups, count, HD), (1, 2, 0, 3))]
where the time goes in v2:
time: 286 us
  Pallas kernels  256 us (90%)
  matrix products  22.2 us (8%)
  local copies, waits for them, and re-layouts  5.16 us (2%)
    pallas_call x7, Pallas kernels, call(): pl.pallas_call(kernel, out_shape=[jax.ShapeDtypeStruct(shape, dtype) for...  256 us
    dot_general x8, matrix products, dot(): lax.dot_general(a, b, (((ca,), (cb,)), ((), ())), preferred_element_type=...  22.2 us

profile of v2, /device:TPU:25, one launch (start us, length us, event | category | flops | bytes accessed | tf_op | source)
XLA Modules:
  0.0 285.7 jit_solution(15002864317132539212)
XLA Ops:
  0.6 0.0 copy-start
  0.7 0.8 constant_dynamic-slice_fusion
  1.5 0.0 copy-start.1
  1.5 1.2 copy-done.1
  2.7 0.0 copy-start.2
  2.7 1.2 copy-done.2
  3.9 15.1 %shard_map.76 = bf16[4,128,1024]{2,1,0:T(8,128)(2,1)S(1)} custom-call(bf16[128,4096]{1,0:T(8,128)(2,1)S(1)} %bitcast.76, bf16[128,4096]{1,0:T(8,128)(2,1)S(1)} %bitcast.77), custom_call_target="tpu_custom_call" | custom-call | tf_op jit(solution)/shard_map/pallas_call | solution.py:55
  19.1 1.3 fusion.18
  20.4 0.0 copy-done
  20.4 2.2 fusion.32
  22.6 4.3 %fusion.14 = bf16[512,1536]{1,0:T(8,128)(2,1)S(1)} fusion(bf16[512,1024]{1,0:T(8,128)(2,1)} %bitcast.85, bf16[1,1024,1536]{2,1,0:T(8,128)(2,1)} %param.7, bf16[512,1024]{1,0:T(8,128)(2,1)} %fusion.32, pred[]{:T(512)S(6)} %eq.3), kind=kOutput, calls=%fused_computation.12 | convolution fusion | flops 1612185600 | bytes 6815745 | tf_op jit(solution)/shard_map/dot_general | solution.py:19
  26.9 60.1 %shard_map.77 = (bf16[128,1536]{1,0:T(8,128)(2,1)S(1)}, bf16[128,1536]{1,0:T(8,128)(2,1)S(1)}, f32[8,128]{1,0:T(8,128)S(1)}, bf16[4,128,1024]{2,1,0:T(8,128)(2,1)S(1)}) custom-call(bf16[4,128,1536]{2,1,0:T(8,128)(2,1)S(1)} %bitcast.74, f32[4,8,128]{2,1,0:T(8,128)S(1)} %broadcast_in_dim.8.refs_1_), custom_call_target="tpu_custom_call" | custom-call | tf_op jit(solution)/shard_map/pallas_call | solution.py:55
  87.1 0.0 copy-start.3
  87.1 0.0 copy-start.6
  87.1 2.3 fusion.35
  89.4 0.0 copy-done.3
  89.4 0.0 copy-done.6
  89.4 0.0 copy-start.5
  89.4 1.2 copy-done.5
  90.6 0.0 copy-start.8
  90.6 19.5 %shard_map.78 = bf16[4,128,1024]{2,1,0:T(8,128)(2,1)S(1)} custom-call(bf16[4,128,1024]{2,1,0:T(8,128)(2,1)S(1)} %bitcast.80, bf16[128,1024]{1,0:T(8,128)(2,1)S(1)} %dynamic-slice_bitcast_fusion.refs_1_), custom_call_target="tpu_custom_call" | custom-call | tf_op jit(solution)/shard_map/pallas_call | solution.py:55
  110.2 0.4 multiply_reduce_fusion
  110.6 0.0 copy-done.8
  110.6 0.0 copy-start.7
  110.6 1.8 fusion.11
  112.4 0.0 copy-done.7
  112.4 71.8 %shard_map.79 = (bf16[4,128,1536]{2,1,0:T(8,128)(2,1)S(1)}, f32[4,8,128]{2,1,0:T(8,128)S(1)}, bf16[128,1024]{1,0:T(8,128)(2,1)S(1)}) custom-call(bf16[4,128,1536]{2,1,0:T(8,128)(2,1)S(1)} %bitcast.75, f32[4,8,128]{2,1,0:T(8,128)S(1)} %broadcast_in_dim.18.refs_1_, bf16[128,1536]{1,0:T(8,128)(2,1)S(1)} %copy-done.7), custom_call_target="tpu_custom_call" | custom-call | tf_op jit(solution)/shard_map/pallas_call | solution.py:55
  184.3 1.8 fusion.20
  186.1 25.4 %shard_map.80 = (bf16[4,128,1024]{2,1,0:T(8,128)(2,1)S(1)}, bf16[4,128,1024]{2,1,0:T(8,128)(2,1)S(1)}) custom-call(bf16[4,128,1024]{2,1,0:T(8,128)(2,1)S(1)} %bitcast.79, bf16[128,1024]{1,0:T(8,128)(2,1)S(1)} %dynamic-slice_bitcast_fusion.refs_1_, bf16[128,1024]{1,0:T(8,128)(2,1)S(1)} %get-tuple-element.16.refs_2_), custom_call_target="tpu_custom_call" | custom-call | tf_op jit(solution)/shard_map/pallas_call | solution.py:55
  211.5 1.5 fusion.38
  213.0 57.5 %shard_map.81 = bf16[4,128,1536]{2,1,0:T(8,128)(2,1)S(1)} custom-call(bf16[4,128,1024]{2,1,0:T(8,128)(2,1)S(1)} %bitcast.81, bf16[128,1536]{1,0:T(8,128)(2,1)S(1)} %get-tuple-element.18.refs_1_, f32[8,128]{1,0:T(8,128)S(1)} %get-tuple-element.19.refs_2_), custom_call_target="tpu_custom_call" | custom-call | tf_op jit(solution)/shard_map/pallas_call | solution.py:55
  270.5 0.0 copy-start.4
  270.5 4.9 %fusion.1 = (f32[1024]{0:T(1024)S(1)}, f32[1,1024,1536]{2,1,0:T(8,128)}) fusion(bf16[1,1024,1536]{2,1,0:T(8,128)(2,1)S(1)} %copy-done.8, f32[1024]{0:T(1024)S(1)} %bitcast.90, bf16[4,128,1536]{2,1,0:T(8,128)(2,1)S(1)} %shard_map.81, bf16[4,128,1536]{2,1,0:T(8,128)(2,1)S(1)} %get-tuple-element.14, pred[]{:T(512)S(6)} %eq.3, ...), kind=kOutput, calls=%fused_computation.3 | convolution fusion | flops 1618213888 | bytes 14688257 | tf_op jit(solution)/shard_map/dot_general | solution.py:19
  275.5 0.0 copy-done.4
  275.5 3.3 %convolution_bitcast_fusion = f32[1,1024,1024]{2,1,0:T(8,128)} fusion(bf16[4,128,1024]{2,1,0:T(8,128)(2,1)S(1)} %copy-done.4, bf16[4,128,1024]{2,1,0:T(8,128)(2,1)S(1)} %get-tuple-element.20, bf16[4,128,1024]{2,1,0:T(8,128)(2,1)S(1)} %get-tuple-element.17, bf16[4,128,1024]{2,1,0:T(8,128)(2,1)S(1)} %shard_map.76, pred[]{:T(512)S(6)} %eq.3), kind=kOutput, calls=%fused_computation.15 | convolution fusion | flops 1074790400 | bytes 8388609 | tf_op jit(solution)/shard_map/dot_general | solution.py:19
  278.8 6.3 %shard_map.82 = f32[8,128]{1,0:T(8,128)S(1)} custom-call(f32[8,128]{1,0:T(8,128)S(1)} %bitcast.83), custom_call_target="tpu_custom_call" | custom-call | tf_op jit(solution)/shard_map/pallas_call | solution.py:55
  285.1 0.6 copy.13
  (4 shorter events, 0.0 us)
Async XLA Ops:
  0.6 19.7 %copy-start = (bf16[1,1024,1024]{2,1,0:T(8,128)(2,1)S(1)}, bf16[1,1024,1024]{2,1,0:T(8,128)(2,1)}, u32[]{:S(2)}) copy-start(bf16[1,1024,1024]{2,1,0:T(8,128)(2,1)} %param.8) | copy-start | bytes 6291460
  1.5 1.2 copy-start.1
  2.7 1.2 copy-start.2
  87.1 2.3 copy-start.3
  87.1 2.3 copy-start.6
  89.4 1.2 copy-start.5
  90.6 19.9 %copy-start.8 = (bf16[1,1024,1536]{2,1,0:T(8,128)(2,1)S(1)}, bf16[1,1024,1536]{2,1,0:T(8,128)(2,1)}, u32[]{:S(2)}) copy-start(bf16[1,1024,1536]{2,1,0:T(8,128)(2,1)} %param.7) | copy-start | bytes 9437188
  110.6 1.8 copy-start.7
  270.5 4.9 %copy-start.4 = (bf16[4,128,1024]{2,1,0:T(8,128)(2,1)S(1)}, bf16[4,128,1024]{2,1,0:T(8,128)(2,1)}, u32[]{:S(2)}) copy-start(bf16[4,128,1024]{2,1,0:T(8,128)(2,1)} %copy-done.3) | copy-start | bytes 3145732

commit v3 on v2

--- a/solution.py
+++ b/solution.py
@@ -216,66 +216,87 @@
     return raised / jnp.sum(raised, axis=-1, keepdims=True)
 
 
-def stage_kernel(mode, count, model, *refs):
+def expect(dst, sems, place, peer, left=False):
+    copy = pltpu.make_async_remote_copy(
+        src_ref=dst,
+        dst_ref=dst,
+        send_sem=sems.at[(0, *place)],
+        recv_sem=sems.at[(1, *place)],
+        device_id=peer,
+        device_id_type=MESH,
+    )
+    if left:
+        copy.wait_send()
+    else:
+        copy.wait_recv()
+
+
+def stage_kernel(mode, owner, count, model, *refs):
     if mode == "forward":
-        part, stat, raw_out, proj, stat_out, result, landed, stats, scatter, gather, small = refs
+        part, stat, raw_out, proj, stat_out, result, landed, stats, scatter, gather, via, small, fanned = refs
     elif mode == "both":
-        part, stat, grads, result, coef_out, mixed_out, landed, stats, proj, scatter, gather, small = refs
+        part, stat, grads, result, coef_out, mixed_out = refs[:6]
+        landed, stats, proj, scatter, gather, via, small, hops, lands, fanned = refs[6:]
     else:
-        part, proj, stat, result, landed, probs_all, scatter, gather = refs
+        part, proj, stat, result, landed, probs_all, scatter, gather, via, hops, lands, fanned = refs
     me = lax.axis_index("dp")
+    section = lax.axis_index("pipe")
+    mine = section == owner
+    partner = {"pipe": 1 - section}
     peers = others("dp")
-    meet([{"dp": p} for p in peers])
+    meet([{"dp": p} for p in peers] + [partner])
     groups = scatter.shape[1]
     seq = part.shape[1]
     cols = part.shape[2] // groups
     full = (GROUP + 2) * HD
     low = GROUP * HD
-    copies, arrivals, ends, stat_copies = [], [], [], []
-    if mode != "backward":
-        for step, peer in enumerate(peers, 1):
-            stat_copies.append(push(stat.at[peer], stats.at[step], small, (0, step), {"dp": peer}))
-    for g in range(groups):
+    last = groups - 1
+    steps = list(range(1, count))
+    last_part = pl.ds(last * cols, cols)
+    last_out = pl.ds(last * low, low) if mode == "forward" else pl.ds(last * full, full)
+    copies = []
+
+    def scatter_direct(g):
         strip = pl.ds(g * cols, cols)
-        arrivals.append(
-            [
-                push(part.at[peer, :, strip], landed.at[step, :, strip], scatter, (g, step), {"dp": peer})
-                for step, peer in enumerate(peers, 1)
-            ]
-        )
-    if mode == "backward":
-        recip = lax.rsqrt(column(stat[0:1, :]) / model + EPSILON)
-        for g in range(groups):
-            for j in range(GROUP):
-                query, key = proj[:, head(g * (GROUP + 2) + j)], proj[:, head(g * (GROUP + 2) + GROUP)]
-                probs_all[g * GROUP + j] = probs_of(query, key)
-    else:
+        for step, peer in enumerate(peers, 1):
+            block = part.at[peer, :, strip]
+            copies.append(push(block, landed.at[step, :, strip], scatter, (g, step), {"dp": peer}))
+
+    def take_stats():
         squares = stat[me]
-        for step, copy in enumerate(stat_copies, 1):
-            copy.wait_recv()
+        for step, peer in enumerate(peers, 1):
+            expect(stats.at[step], small, (0, step), {"dp": peer})
             squares = squares + stats[step]
-        recip = lax.rsqrt(column(squares[0:1, :]) / model + EPSILON)
-        if mode == "forward":
-            stat_out[...] = squares
-    coef = jnp.zeros((seq, 1), F32)
-    for g in range(groups):
+        return squares
+
+    def send_stats():
+        for step, peer in enumerate(peers, 1):
+            copies.append(push(stat.at[peer], stats.at[step], small, (0, step), {"dp": peer}))
+
+    def arrived(g):
+        strip = pl.ds(g * cols, cols)
+        for step, peer in enumerate(peers, 1):
+            if g == last and mode != "forward":
+                expect(landed.at[step, :, strip], via, (2, step), partner)
+            else:
+                expect(landed.at[step, :, strip], scatter, (g, step), {"dp": peer})
+
+    def total(at):
+        sums = part[me, :, at].astype(F32)
+        for step in steps:
+            sums = sums + landed[step, :, at].astype(F32)
+        return sums
+
+    def project(g, recip):
+        for i in range(GROUP + 2):
+            at = pl.ds(g * full + i * HD, HD)
+            raw = total(at)
+            if mode == "forward":
+                raw_out[:, at] = raw.astype(BF)
+            proj[:, at] = (raw * recip).astype(BF)
+
+    def work(g, recip, coef):
         base = g * full
-        for copy in arrivals[g]:
-            copy.wait_recv()
-
-        def total(at):
-            sums = part[me, :, at].astype(F32)
-            for step in range(1, count):
-                sums = sums + landed[step, :, at].astype(F32)
-            return sums
-
-        if mode != "backward":
-            for i in range(GROUP + 2):
-                at = pl.ds(base + i * HD, HD)
-                raw = total(at)
-                if mode == "forward":
-                    raw_out[:, at] = raw.astype(BF)
-                proj[:, at] = (raw * recip).astype(BF)
         key, value = proj[:, pl.ds(base + low, HD)], proj[:, pl.ds(base + low + HD, HD)]
         grad_key = jnp.zeros((seq, HD), F32)
         grad_value = jnp.zeros((seq, HD), F32)
@@ -313,40 +334,142 @@
             if mode == "both":
                 coef = coef + jnp.sum(grad_key * key.astype(F32), axis=-1, keepdims=True)
                 coef = coef + jnp.sum(grad_value * value.astype(F32), axis=-1, keepdims=True)
-        for step, peer in enumerate(peers, 1):
-            block = result.at[me, :, strip]
-            ends.append(push(block, block, gather, (g, step), {"dp": peer}))
-    if mode == "both":
-        coef_out[me] = jnp.broadcast_to(as_row(coef * recip * recip / model), coef_out.shape[1:])
-        for step, peer in enumerate(peers, 1):
-            block = coef_out.at[me]
-            ends.append(push(block, block, small, (1, step), {"dp": peer}))
-    for copy in ends:
-        copy.wait()
-    for copy in sum(arrivals, stat_copies):
-        copy.wait_send()
-
-
-def stage(mode, arrays, groups, model, collective_id):
+        block = result.at[me, :, strip]
+        if g == last:
+            push(block, fanned.at[0], via, (3, 0), partner)
+        else:
+            for step, peer in enumerate(peers, 1):
+                push(block, block, gather, (g, step), {"dp": peer})
+        return coef
+
+    def collect():
+        for g in range(last):
+            strip = pl.ds(g * low, low) if mode == "forward" else pl.ds(g * full, full)
+            for step, peer in enumerate(peers, 1):
+                source = lax.rem(me + count - step, count)
+                expect(result.at[source, :, strip], gather, (g, step), {"dp": peer})
+        for step in steps:
+            source = lax.rem(me + count - step, count)
+            expect(result.at[source, :, last_out], via, (5, step), partner)
+        for g in range(last):
+            strip = pl.ds(g * low, low) if mode == "forward" else pl.ds(g * full, full)
+            for step, peer in enumerate(peers, 1):
+                expect(result.at[me, :, strip], gather, (g, step), {"dp": peer}, True)
+        expect(result.at[me, :, last_out], via, (3, 0), partner, True)
+
+    def help_gather():
+        sent = []
+        expect(fanned.at[0], via, (3, 0), partner)
+        for step, peer in enumerate(peers, 1):
+            sent.append(push(fanned.at[0], fanned.at[step], via, (4, step), {"dp": peer}))
+        for step, peer in enumerate(peers, 1):
+            source = lax.rem(me + count - step, count)
+            expect(fanned.at[step], via, (4, step), {"dp": peer})
+            sent.append(push(fanned.at[step], result.at[source, :, last_out], via, (5, step), partner))
+        for copy in sent:
+            copy.wait_send()
+
+    if mode == "forward":
+        send_stats()
+        for g in range(groups):
+            scatter_direct(g)
+        squares = take_stats()
+        stat_out[...] = squares
+        recip = lax.rsqrt(column(squares[0:1, :]) / model + EPSILON)
+        for g in range(groups):
+            arrived(g)
+            project(g, recip)
+
+            @pl.when(mine)
+            def attention(g=g):
+                work(g, recip, None)
+
+        pl.when(mine)(collect)
+        pl.when(section != owner)(help_gather)
+        for copy in copies:
+            copy.wait_send()
+        return
+
+    @pl.when(mine)
+    def owning():
+        if mode == "both":
+            send_stats()
+        for step, peer in enumerate(peers, 1):
+            copies.append(push(part.at[peer, :, last_part], hops.at[step], via, (0, step), partner))
+        for g in range(last):
+            scatter_direct(g)
+        if mode == "backward":
+            squares = stat[...]
+            for g in range(groups):
+                key = proj[:, pl.ds(g * full + low, HD)]
+                for j in range(GROUP):
+                    probs_all[g * GROUP + j] = probs_of(proj[:, pl.ds(g * full + j * HD, HD)], key)
+        else:
+            squares = take_stats()
+        recip = lax.rsqrt(column(squares[0:1, :]) / model + EPSILON)
+        coef = jnp.zeros((seq, 1), F32)
+        sent = []
+        for g in range(groups):
+            arrived(g)
+            if mode == "both":
+                project(g, recip)
+            coef = work(g, recip, coef)
+        if mode == "both":
+            coef_out[me] = jnp.broadcast_to(as_row(coef * recip * recip / model), coef_out.shape[1:])
+            for step, peer in enumerate(peers, 1):
+                block = coef_out.at[me]
+                sent.append(push(block, block, small, (1, step), {"dp": peer}))
+            for step, peer in enumerate(peers, 1):
+                source = lax.rem(me + count - step, count)
+                expect(coef_out.at[source], small, (1, step), {"dp": peer})
+        collect()
+        for copy in copies + sent:
+            copy.wait_send()
+
+    @pl.when(section != owner)
+    def helping():
+        passed = []
+
+        def onward(step):
+            expect(hops.at[step], via, (0, step), partner)
+            passed.append(push(hops.at[step], lands.at[step], via, (1, step), {"dp": peers[step - 1]}))
+
+        def home(step):
+            expect(lands.at[step], via, (1, step), {"dp": peers[step - 1]})
+            passed.append(push(lands.at[step], landed.at[step, :, last_part], via, (2, step), partner))
+
+        onward(1)
+        for step in steps:
+            if step + 1 < count:
+                onward(step + 1)
+            home(step)
+        for copy in passed:
+            copy.wait_send()
+        help_gather()
+
+
+def stage(mode, owner, arrays, groups, model, collective_id):
     part = arrays[0]
     count, seq, cols = part.shape
     full = groups * (GROUP + 2) * HD
     low = groups * GROUP * HD
     dma = pltpu.SemaphoreType.DMA
-    sems = [dma((2, groups, count)), dma((2, groups, count))]
+    sems = [dma((2, groups, count)), dma((2, groups, count)), dma((2, 6, count))]
     landed = pltpu.VMEM(part.shape, BF)
+    hop = pltpu.VMEM((count, seq, cols // groups), BF)
+    fanned = pltpu.VMEM((count, seq, (low if mode == "forward" else full) // groups), BF)
+    stats = pltpu.VMEM((count, 8, seq), F32)
     if mode == "backward":
         outs = [((count, seq, full), BF)]
-        scratch = [landed, pltpu.VMEM((groups * GROUP, seq, seq), F32), *sems]
+        scratch = [landed, pltpu.VMEM((groups * GROUP, seq, seq), F32), *sems, hop, hop, fanned]
+    elif mode == "forward":
+        outs = [((seq, full), BF), ((seq, full), BF), ((8, seq), F32), ((count, seq, low), BF)]
+        scratch = [landed, stats, *sems, dma((2, 2, count)), fanned]
     else:
-        stats = pltpu.VMEM((count, 8, seq), F32)
-        if mode == "forward":
-            outs = [((seq, full), BF), ((seq, full), BF), ((8, seq), F32), ((count, seq, low), BF)]
-            scratch = [landed, stats, *sems, dma((2, 2, count))]
-        else:
-            outs = [((count, seq, full), BF), ((count, 8, seq), F32), ((seq, low), BF)]
-            scratch = [landed, stats, pltpu.VMEM((seq, full), BF), *sems, dma((2, 2, count))]
-    return call(functools.partial(stage_kernel, mode, count, model), collective_id, arrays, outs, scratch)
+        outs = [((count, seq, full), BF), ((count, 8, seq), F32), ((seq, low), BF)]
+        scratch = [landed, stats, pltpu.VMEM((seq, full), BF), *sems, dma((2, 2, count)), hop, hop, fanned]
+    kernel = functools.partial(stage_kernel, mode, owner, count, model)
+    return call(kernel, collective_id, arrays, outs, scratch)
 
 
 def total_kernel(count, in_ref, out_ref, landed, sems):
@@ -392,20 +515,20 @@
     proj_part, squares = project(held)
     mixed_part = jnp.pad(dot(held, out, 1, 0).astype(BF), ((0, 0), (0, cols - head_cols)))
     part = jnp.where(first, proj_part, mixed_part).reshape(count, seq, cols)
-    grads, proj, squares, mixed_start = stage("forward", [part, squares], groups, model, 1)
+    grads, proj, squares, mixed_start = stage("forward", 0, [part, squares], groups, model, 1)
     mixed_start = mixed_start.reshape(rows, head_cols)
     carried = relay(dot(mixed_start, out, 1, 1).astype(BF), held, 2)
 
     part, next_squares = project(carried)
     part = part.reshape(count, seq, cols)
-    grad_proj_next, coef, mixed = stage("both", [part, next_squares, grads], groups, model, 3)
+    grad_proj_next, coef, mixed = stage("both", 1, [part, next_squares, grads], groups, model, 3)
     grad_proj_next = grad_proj_next.reshape(rows, cols)
     coef = coef[:, 0].reshape(rows, 1)
     back = dot(grad_proj_next, qkv, 1, 1) * gain - carried.astype(F32) * coef
     returned, mixed_next = relay(back.astype(BF), held, 4, mixed)
 
     part = dot(returned, out, 1, 0).astype(BF).reshape(count, seq, head_cols)
-    (grad_proj,) = stage("backward", [part, proj, squares], groups, model, 5)
+    (grad_proj,) = stage("backward", 0, [part, proj, squares], groups, model, 5)
 
     block_in = jnp.where(first, held, carried)
     grad_out = jnp.where(first, returned, held)

time: 286 us -> 275 us (0.962)
  Pallas kernels: 256 us -> 245 us
    pallas_call x7, Pallas kernels: 256 us -> 245 us  [call(): pl.pallas_call(kernel, out_shape=[jax.ShapeDtypeStruct(shape, dtype) for...]
where the time goes in v3:
time: 275 us
  Pallas kernels  245 us (89%)
  matrix products  22 us (8%)
  local copies, waits for them, and re-layouts  5.16 us (2%)
    pallas_call x7, Pallas kernels, call(): pl.pallas_call(kernel, out_shape=[jax.ShapeDtypeStruct(shape, dtype) for...  245 us
    dot_general x8, matrix products, dot(): lax.dot_general(a, b, (((ca,), (cb,)), ((), ())), preferred_element_type=...  22 us

profile of v3, /device:TPU:25, one launch (start us, length us, event | category | flops | bytes accessed | tf_op | source)
XLA Modules:
  0.0 275.1 jit_solution(17912971435400278276)
XLA Ops:
  0.6 0.0 copy-start
  0.7 0.8 constant_dynamic-slice_fusion
  1.5 0.0 copy-start.1
  1.5 1.2 copy-done.1
  2.7 0.0 copy-start.2
  2.7 1.2 copy-done.2
  3.9 15.1 %shard_map.76 = bf16[4,128,1024]{2,1,0:T(8,128)(2,1)S(1)} custom-call(bf16[128,4096]{1,0:T(8,128)(2,1)S(1)} %bitcast.76, bf16[128,4096]{1,0:T(8,128)(2,1)S(1)} %bitcast.77), custom_call_target="tpu_custom_call" | custom-call | tf_op jit(solution)/shard_map/pallas_call | solution.py:55
  19.1 1.3 fusion.18
  20.4 0.0 copy-done
  20.4 2.2 fusion.32
  22.6 4.3 %fusion.14 = bf16[512,1536]{1,0:T(8,128)(2,1)S(1)} fusion(bf16[512,1024]{1,0:T(8,128)(2,1)} %bitcast.85, bf16[1,1024,1536]{2,1,0:T(8,128)(2,1)} %param.7, bf16[512,1024]{1,0:T(8,128)(2,1)} %fusion.32, pred[]{:T(512)S(6)} %eq.3), kind=kOutput, calls=%fused_computation.12 | convolution fusion | flops 1612185600 | bytes 6815745 | tf_op jit(solution)/shard_map/dot_general | solution.py:19
  26.9 64.0 %shard_map.77 = (bf16[128,1536]{1,0:T(8,128)(2,1)S(1)}, bf16[128,1536]{1,0:T(8,128)(2,1)S(1)}, f32[8,128]{1,0:T(8,128)S(1)}, bf16[4,128,1024]{2,1,0:T(8,128)(2,1)S(1)}) custom-call(bf16[4,128,1536]{2,1,0:T(8,128)(2,1)S(1)} %bitcast.74, f32[4,8,128]{2,1,0:T(8,128)S(1)} %broadcast_in_dim.8.refs_1_), custom_call_target="tpu_custom_call" | custom-call | tf_op jit(solution)/shard_map/pallas_call | solution.py:55
  90.9 0.0 copy-start.3
  90.9 0.0 copy-start.6
  91.0 2.3 fusion.35
  93.2 0.0 copy-done.3
  93.2 0.0 copy-done.6
  93.3 0.0 copy-start.5
  93.3 1.2 copy-done.5
  94.5 0.0 copy-start.8
  94.5 20.2 %shard_map.78 = bf16[4,128,1024]{2,1,0:T(8,128)(2,1)S(1)} custom-call(bf16[4,128,1024]{2,1,0:T(8,128)(2,1)S(1)} %bitcast.80, bf16[128,1024]{1,0:T(8,128)(2,1)S(1)} %dynamic-slice_bitcast_fusion.refs_1_), custom_call_target="tpu_custom_call" | custom-call | tf_op jit(solution)/shard_map/pallas_call | solution.py:55
  114.7 0.4 multiply_reduce_fusion
  115.1 0.0 copy-done.8
  115.1 0.0 copy-start.7
  115.1 1.8 fusion.11
  117.0 0.0 copy-done.7
  117.0 63.6 %shard_map.79 = (bf16[4,128,1536]{2,1,0:T(8,128)(2,1)S(1)}, f32[4,8,128]{2,1,0:T(8,128)S(1)}, bf16[128,1024]{1,0:T(8,128)(2,1)S(1)}) custom-call(bf16[4,128,1536]{2,1,0:T(8,128)(2,1)S(1)} %bitcast.75, f32[4,8,128]{2,1,0:T(8,128)S(1)} %broadcast_in_dim.18.refs_1_, bf16[128,1536]{1,0:T(8,128)(2,1)S(1)} %copy-done.7), custom_call_target="tpu_custom_call" | custom-call | tf_op jit(solution)/shard_map/pallas_call | solution.py:55
  180.6 1.8 fusion.20
  182.5 23.0 %shard_map.80 = (bf16[4,128,1024]{2,1,0:T(8,128)(2,1)S(1)}, bf16[4,128,1024]{2,1,0:T(8,128)(2,1)S(1)}) custom-call(bf16[4,128,1024]{2,1,0:T(8,128)(2,1)S(1)} %bitcast.79, bf16[128,1024]{1,0:T(8,128)(2,1)S(1)} %dynamic-slice_bitcast_fusion.refs_1_, bf16[128,1024]{1,0:T(8,128)(2,1)S(1)} %get-tuple-element.16.refs_2_), custom_call_target="tpu_custom_call" | custom-call | tf_op jit(solution)/shard_map/pallas_call | solution.py:55
  205.5 1.3 fusion.38
  206.8 53.9 %shard_map.81 = bf16[4,128,1536]{2,1,0:T(8,128)(2,1)S(1)} custom-call(bf16[4,128,1024]{2,1,0:T(8,128)(2,1)S(1)} %bitcast.81, bf16[128,1536]{1,0:T(8,128)(2,1)S(1)} %get-tuple-element.18.refs_1_, f32[8,128]{1,0:T(8,128)S(1)} %get-tuple-element.19.refs_2_), custom_call_target="tpu_custom_call" | custom-call | tf_op jit(solution)/shard_map/pallas_call | solution.py:55
  260.7 0.0 copy-start.4
  260.7 4.9 %fusion.1 = (f32[1024]{0:T(1024)S(1)}, f32[1,1024,1536]{2,1,0:T(8,128)}) fusion(bf16[1,1024,1536]{2,1,0:T(8,128)(2,1)S(1)} %copy-done.8, f32[1024]{0:T(1024)S(1)} %bitcast.90, bf16[4,128,1536]{2,1,0:T(8,128)(2,1)S(1)} %shard_map.81, bf16[4,128,1536]{2,1,0:T(8,128)(2,1)S(1)} %get-tuple-element.14, pred[]{:T(512)S(6)} %eq.3, ...), kind=kOutput, calls=%fused_computation.3 | convolution fusion | flops 1618213888 | bytes 14688257 | tf_op jit(solution)/shard_map/dot_general | solution.py:19
  265.7 0.0 copy-done.4
  265.7 3.3 %convolution_bitcast_fusion = f32[1,1024,1024]{2,1,0:T(8,128)} fusion(bf16[4,128,1024]{2,1,0:T(8,128)(2,1)S(1)} %copy-done.4, bf16[4,128,1024]{2,1,0:T(8,128)(2,1)S(1)} %get-tuple-element.20, bf16[4,128,1024]{2,1,0:T(8,128)(2,1)S(1)} %get-tuple-element.17, bf16[4,128,1024]{2,1,0:T(8,128)(2,1)S(1)} %shard_map.76, pred[]{:T(512)S(6)} %eq.3), kind=kOutput, calls=%fused_computation.15 | convolution fusion | flops 1074790400 | bytes 8388609 | tf_op jit(solution)/shard_map/dot_general | solution.py:19
  269.0 5.5 %shard_map.82 = f32[8,128]{1,0:T(8,128)S(1)} custom-call(f32[8,128]{1,0:T(8,128)S(1)} %bitcast.83), custom_call_target="tpu_custom_call" | custom-call | tf_op jit(solution)/shard_map/pallas_call | solution.py:55
  274.5 0.6 copy.13
  (4 shorter events, 0.0 us)
Async XLA Ops:
  0.6 19.7 %copy-start = (bf16[1,1024,1024]{2,1,0:T(8,128)(2,1)S(1)}, bf16[1,1024,1024]{2,1,0:T(8,128)(2,1)}, u32[]{:S(2)}) copy-start(bf16[1,1024,1024]{2,1,0:T(8,128)(2,1)} %param.8) | copy-start | bytes 6291460
  1.5 1.2 copy-start.1
  2.7 1.2 copy-start.2
  90.9 2.3 copy-start.3
  90.9 2.3 copy-start.6
  93.3 1.2 copy-start.5
  94.5 20.6 %copy-start.8 = (bf16[1,1024,1536]{2,1,0:T(8,128)(2,1)S(1)}, bf16[1,1024,1536]{2,1,0:T(8,128)(2,1)}, u32[]{:S(2)}) copy-start(bf16[1,1024,1536]{2,1,0:T(8,128)(2,1)} %param.7) | copy-start | bytes 9437188
  115.1 1.8 copy-start.7
  260.7 5.0 %copy-start.4 = (bf16[4,128,1024]{2,1,0:T(8,128)(2,1)S(1)}, bf16[4,128,1024]{2,1,0:T(8,128)(2,1)}, u32[]{:S(2)}) copy-start(bf16[4,128,1024]{2,1,0:T(8,128)(2,1)} %copy-done.3) | copy-start | bytes 3145732

commit v4 on v3

--- a/solution.py
+++ b/solution.py
@@ -10,6 +10,7 @@
 HD = 128
 GROUP = 4
 EPSILON = 1e-05
+PIECES = 2
 BF = jnp.bfloat16
 F32 = jnp.float32
 MESH = pl.DeviceIdType.MESH
@@ -233,7 +234,7 @@
 
 def stage_kernel(mode, owner, count, model, *refs):
     if mode == "forward":
-        part, stat, raw_out, proj, stat_out, result, landed, stats, scatter, gather, via, small, fanned = refs
+        part, stat, raw_out, proj, stat_out, result, landed, stats, scatter, gather, via, small = refs
     elif mode == "both":
         part, stat, grads, result, coef_out, mixed_out = refs[:6]
         landed, stats, proj, scatter, gather, via, small, hops, lands, fanned = refs[6:]
@@ -252,6 +253,8 @@
     low = GROUP * HD
     last = groups - 1
     steps = list(range(1, count))
+    direct = groups if mode == "forward" else last
+    pieces = [(i, pl.ds(i * (seq // PIECES), seq // PIECES)) for i in range(PIECES)]
     last_part = pl.ds(last * cols, cols)
     last_out = pl.ds(last * low, low) if mode == "forward" else pl.ds(last * full, full)
     copies = []
@@ -277,7 +280,8 @@
         strip = pl.ds(g * cols, cols)
         for step, peer in enumerate(peers, 1):
             if g == last and mode != "forward":
-                expect(landed.at[step, :, strip], via, (2, step), partner)
+                for i, cut in pieces:
+                    expect(landed.at[step, cut, strip], via, (2, step, i), partner)
             else:
                 expect(landed.at[step, :, strip], scatter, (g, step), {"dp": peer})
 
@@ -335,37 +339,43 @@
                 coef = coef + jnp.sum(grad_key * key.astype(F32), axis=-1, keepdims=True)
                 coef = coef + jnp.sum(grad_value * value.astype(F32), axis=-1, keepdims=True)
         block = result.at[me, :, strip]
-        if g == last:
-            push(block, fanned.at[0], via, (3, 0), partner)
+        if g >= direct:
+            for i, cut in pieces:
+                push(result.at[me, cut, strip], fanned.at[0, cut], via, (3, 0, i), partner)
         else:
             for step, peer in enumerate(peers, 1):
                 push(block, block, gather, (g, step), {"dp": peer})
         return coef
 
     def collect():
-        for g in range(last):
+        for g in range(direct):
             strip = pl.ds(g * low, low) if mode == "forward" else pl.ds(g * full, full)
             for step, peer in enumerate(peers, 1):
                 source = lax.rem(me + count - step, count)
                 expect(result.at[source, :, strip], gather, (g, step), {"dp": peer})
-        for step in steps:
+        for step in steps if direct < groups else []:
             source = lax.rem(me + count - step, count)
-            expect(result.at[source, :, last_out], via, (5, step), partner)
-        for g in range(last):
+            for i, cut in pieces:
+                expect(result.at[source, cut, last_out], via, (5, step, i), partner)
+        for g in range(direct):
             strip = pl.ds(g * low, low) if mode == "forward" else pl.ds(g * full, full)
             for step, peer in enumerate(peers, 1):
                 expect(result.at[me, :, strip], gather, (g, step), {"dp": peer}, True)
-        expect(result.at[me, :, last_out], via, (3, 0), partner, True)
+        for i, cut in pieces if direct < groups else []:
+            expect(result.at[me, cut, last_out], via, (3, 0, i), partner, True)
 
     def help_gather():
         sent = []
-        expect(fanned.at[0], via, (3, 0), partner)
-        for step, peer in enumerate(peers, 1):
-            sent.append(push(fanned.at[0], fanned.at[step], via, (4, step), {"dp": peer}))
-        for step, peer in enumerate(peers, 1):
-            source = lax.rem(me + count - step, count)
-            expect(fanned.at[step], via, (4, step), {"dp": peer})
-            sent.append(push(fanned.at[step], result.at[source, :, last_out], via, (5, step), partner))
+        for i, cut in pieces:
+            expect(fanned.at[0, cut], via, (3, 0, i), partner)
+            for step, peer in enumerate(peers, 1):
+                sent.append(push(fanned.at[0, cut], fanned.at[step, cut], via, (4, step, i), {"dp": peer}))
+        for i, cut in pieces:
+            for step, peer in enumerate(peers, 1):
+                source = lax.rem(me + count - step, count)
+                expect(fanned.at[step, cut], via, (4, step, i), {"dp": peer})
+                home = result.at[source, cut, last_out]
+                sent.append(push(fanned.at[step, cut], home, via, (5, step, i), partner))
         for copy in sent:
             copy.wait_send()
 
@@ -385,7 +395,6 @@
                 work(g, recip, None)
 
         pl.when(mine)(collect)
-        pl.when(section != owner)(help_gather)
         for copy in copies:
             copy.wait_send()
         return
@@ -395,7 +404,9 @@
         if mode == "both":
             send_stats()
         for step, peer in enumerate(peers, 1):
-            copies.append(push(part.at[peer, :, last_part], hops.at[step], via, (0, step), partner))
+            for i, cut in pieces:
+                block = part.at[peer, cut, last_part]
+                copies.append(push(block, hops.at[step, cut], via, (0, step, i), partner))
         for g in range(last):
             scatter_direct(g)
         if mode == "backward":
@@ -430,19 +441,24 @@
     def helping():
         passed = []
 
-        def onward(step):
-            expect(hops.at[step], via, (0, step), partner)
-            passed.append(push(hops.at[step], lands.at[step], via, (1, step), {"dp": peers[step - 1]}))
-
-        def home(step):
-            expect(lands.at[step], via, (1, step), {"dp": peers[step - 1]})
-            passed.append(push(lands.at[step], landed.at[step, :, last_part], via, (2, step), partner))
-
-        onward(1)
-        for step in steps:
-            if step + 1 < count:
-                onward(step + 1)
-            home(step)
+        def onward(step, i, cut):
+            expect(hops.at[step, cut], via, (0, step, i), partner)
+            peer = {"dp": peers[step - 1]}
+            passed.append(push(hops.at[step, cut], lands.at[step, cut], via, (1, step, i), peer))
+
+        def home(step, i, cut):
+            expect(lands.at[step, cut], via, (1, step, i), {"dp": peers[step - 1]})
+            block = landed.at[step, cut, last_part]
+            passed.append(push(lands.at[step, cut], block, via, (2, step, i), partner))
+
+        order = [(step, i, cut) for step in steps for i, cut in pieces]
+        ahead = min(2, len(order))
+        for item in order[:ahead]:
+            onward(*item)
+        for index, item in enumerate(order):
+            if index + ahead < len(order):
+                onward(*order[index + ahead])
+            home(*item)
         for copy in passed:
             copy.wait_send()
         help_gather()
@@ -454,7 +470,7 @@
     full = groups * (GROUP + 2) * HD
     low = groups * GROUP * HD
     dma = pltpu.SemaphoreType.DMA
-    sems = [dma((2, groups, count)), dma((2, groups, count)), dma((2, 6, count))]
+    sems = [dma((2, groups, count)), dma((2, groups, count)), dma((2, 6, count, PIECES))]
     landed = pltpu.VMEM(part.shape, BF)
     hop = pltpu.VMEM((count, seq, cols // groups), BF)
     fanned = pltpu.VMEM((count, seq, (low if mode == "forward" else full) // groups), BF)
@@ -464,7 +480,7 @@
         scratch = [landed, pltpu.VMEM((groups * GROUP, seq, seq), F32), *sems, hop, hop, fanned]
     elif mode == "forward":
         outs = [((seq, full), BF), ((seq, full), BF), ((8, seq), F32), ((count, seq, low), BF)]
-        scratch = [landed, stats, *sems, dma((2, 2, count)), fanned]
+        scratch = [landed, stats, *sems, dma((2, 2, count))]
     else:
         outs = [((count, seq, full), BF), ((count, 8, seq), F32), ((seq, low), BF)]
         scratch = [landed, stats, pltpu.VMEM((seq, full), BF), *sems, dma((2, 2, count)), hop, hop, fanned]

time: 275 us -> 256 us (0.931)
  Pallas kernels: 245 us -> 225 us
    pallas_call x7, Pallas kernels: 245 us -> 225 us  [call(): pl.pallas_call(kernel, out_shape=[jax.ShapeDtypeStruct(shape, dtype) for...]
where the time goes in v4:
time: 256 us; the launch traced here: 255 us
  Pallas kernels  225 us (88%)
  matrix products  22 us (9%)
  local copies, waits for them, and re-layouts  5.16 us (2%)
    pallas_call x7, Pallas kernels, call(): pl.pallas_call(kernel, out_shape=[jax.ShapeDtypeStruct(shape, dtype) for...  225 us
    dot_general x8, matrix products, dot(): lax.dot_general(a, b, (((ca,), (cb,)), ((), ())), preferred_element_type=...  22 us

profile of v4, /device:TPU:25, one launch (start us, length us, event | category | flops | bytes accessed | tf_op | source)
XLA Modules:
  0.0 254.9 jit_solution(64560700506323830)
XLA Ops:
  0.6 0.0 copy-start
  0.7 0.8 constant_dynamic-slice_fusion
  1.5 0.0 copy-start.1
  1.5 1.2 copy-done.1
  2.7 0.0 copy-start.2
  2.7 1.2 copy-done.2
  3.9 15.1 %shard_map.76 = bf16[4,128,1024]{2,1,0:T(8,128)(2,1)S(1)} custom-call(bf16[128,4096]{1,0:T(8,128)(2,1)S(1)} %bitcast.76, bf16[128,4096]{1,0:T(8,128)(2,1)S(1)} %bitcast.77), custom_call_target="tpu_custom_call" | custom-call | tf_op jit(solution)/shard_map/pallas_call | solution.py:56
  19.1 1.3 fusion.18
  20.4 0.0 copy-done
  20.4 2.2 fusion.32
  22.6 4.3 %fusion.14 = bf16[512,1536]{1,0:T(8,128)(2,1)S(1)} fusion(bf16[512,1024]{1,0:T(8,128)(2,1)} %bitcast.85, bf16[1,1024,1536]{2,1,0:T(8,128)(2,1)} %param.7, bf16[512,1024]{1,0:T(8,128)(2,1)} %fusion.32, pred[]{:T(512)S(6)} %eq.3), kind=kOutput, calls=%fused_computation.12 | convolution fusion | flops 1612185600 | bytes 6815745 | tf_op jit(solution)/shard_map/dot_general | solution.py:20
  26.9 61.0 %shard_map.77 = (bf16[128,1536]{1,0:T(8,128)(2,1)S(1)}, bf16[128,1536]{1,0:T(8,128)(2,1)S(1)}, f32[8,128]{1,0:T(8,128)S(1)}, bf16[4,128,1024]{2,1,0:T(8,128)(2,1)S(1)}) custom-call(bf16[4,128,1536]{2,1,0:T(8,128)(2,1)S(1)} %bitcast.74, f32[4,8,128]{2,1,0:T(8,128)S(1)} %broadcast_in_dim.8.refs_1_), custom_call_target="tpu_custom_call" | custom-call | tf_op jit(solution)/shard_map/pallas_call | solution.py:56
  87.9 0.0 copy-start.3
  87.9 0.0 copy-start.6
  87.9 2.3 fusion.35
  90.2 0.0 copy-done.3
  90.2 0.0 copy-done.6
  90.2 0.0 copy-start.5
  90.2 1.2 copy-done.5
  91.5 0.0 copy-start.8
  91.5 18.9 %shard_map.78 = bf16[4,128,1024]{2,1,0:T(8,128)(2,1)S(1)} custom-call(bf16[4,128,1024]{2,1,0:T(8,128)(2,1)S(1)} %bitcast.80, bf16[128,1024]{1,0:T(8,128)(2,1)S(1)} %dynamic-slice_bitcast_fusion.refs_1_), custom_call_target="tpu_custom_call" | custom-call | tf_op jit(solution)/shard_map/pallas_call | solution.py:56
  110.4 0.4 multiply_reduce_fusion
  110.8 0.0 copy-done.8
  110.8 0.0 copy-start.7
  110.8 1.8 fusion.11
  112.6 0.0 copy-done.7
  112.6 55.5 %shard_map.79 = (bf16[4,128,1536]{2,1,0:T(8,128)(2,1)S(1)}, f32[4,8,128]{2,1,0:T(8,128)S(1)}, bf16[128,1024]{1,0:T(8,128)(2,1)S(1)}) custom-call(bf16[4,128,1536]{2,1,0:T(8,128)(2,1)S(1)} %bitcast.75, f32[4,8,128]{2,1,0:T(8,128)S(1)} %broadcast_in_dim.18.refs_1_, bf16[128,1536]{1,0:T(8,128)(2,1)S(1)} %copy-done.7), custom_call_target="tpu_custom_call" | custom-call | tf_op jit(solution)/shard_map/pallas_call | solution.py:56
  168.1 1.8 fusion.20
  170.0 24.0 %shard_map.80 = (bf16[4,128,1024]{2,1,0:T(8,128)(2,1)S(1)}, bf16[4,128,1024]{2,1,0:T(8,128)(2,1)S(1)}) custom-call(bf16[4,128,1024]{2,1,0:T(8,128)(2,1)S(1)} %bitcast.79, bf16[128,1024]{1,0:T(8,128)(2,1)S(1)} %dynamic-slice_bitcast_fusion.refs_1_, bf16[128,1024]{1,0:T(8,128)(2,1)S(1)} %get-tuple-element.16.refs_2_), custom_call_target="tpu_custom_call" | custom-call | tf_op jit(solution)/shard_map/pallas_call | solution.py:56
  194.0 1.3 fusion.38
  195.3 38.7 %shard_map.81 = bf16[4,128,1536]{2,1,0:T(8,128)(2,1)S(1)} custom-call(bf16[4,128,1024]{2,1,0:T(8,128)(2,1)S(1)} %bitcast.81, bf16[128,1536]{1,0:T(8,128)(2,1)S(1)} %get-tuple-element.18.refs_1_, f32[8,128]{1,0:T(8,128)S(1)} %get-tuple-element.19.refs_2_), custom_call_target="tpu_custom_call" | custom-call | tf_op jit(solution)/shard_map/pallas_call | solution.py:56
  234.0 0.0 copy-start.4
  234.0 4.9 %fusion.1 = (f32[1024]{0:T(1024)S(1)}, f32[1,1024,1536]{2,1,0:T(8,128)}) fusion(bf16[1,1024,1536]{2,1,0:T(8,128)(2,1)S(1)} %copy-done.8, f32[1024]{0:T(1024)S(1)} %bitcast.90, bf16[4,128,1536]{2,1,0:T(8,128)(2,1)S(1)} %shard_map.81, bf16[4,128,1536]{2,1,0:T(8,128)(2,1)S(1)} %get-tuple-element.14, pred[]{:T(512)S(6)} %eq.3, ...), kind=kOutput, calls=%fused_computation.3 | convolution fusion | flops 1618213888 | bytes 14688257 | tf_op jit(solution)/shard_map/dot_general | solution.py:20
  239.0 0.0 copy-done.4
  239.0 3.3 %convolution_bitcast_fusion = f32[1,1024,1024]{2,1,0:T(8,128)} fusion(bf16[4,128,1024]{2,1,0:T(8,128)(2,1)S(1)} %copy-done.4, bf16[4,128,1024]{2,1,0:T(8,128)(2,1)S(1)} %get-tuple-element.20, bf16[4,128,1024]{2,1,0:T(8,128)(2,1)S(1)} %get-tuple-element.17, bf16[4,128,1024]{2,1,0:T(8,128)(2,1)S(1)} %shard_map.76, pred[]{:T(512)S(6)} %eq.3), kind=kOutput, calls=%fused_computation.15 | convolution fusion | flops 1074790400 | bytes 8388609 | tf_op jit(solution)/shard_map/dot_general | solution.py:20
  242.3 12.0 %shard_map.82 = f32[8,128]{1,0:T(8,128)S(1)} custom-call(f32[8,128]{1,0:T(8,128)S(1)} %bitcast.83), custom_call_target="tpu_custom_call" | custom-call | tf_op jit(solution)/shard_map/pallas_call | solution.py:56
  254.3 0.6 copy.13
  (4 shorter events, 0.0 us)
Async XLA Ops:
  0.6 19.7 %copy-start = (bf16[1,1024,1024]{2,1,0:T(8,128)(2,1)S(1)}, bf16[1,1024,1024]{2,1,0:T(8,128)(2,1)}, u32[]{:S(2)}) copy-start(bf16[1,1024,1024]{2,1,0:T(8,128)(2,1)} %param.8) | copy-start | bytes 6291460
  1.5 1.2 copy-start.1
  2.7 1.2 copy-start.2
  87.9 2.3 copy-start.3
  87.9 2.3 copy-start.6
  90.2 1.2 copy-start.5
  91.5 19.3 %copy-start.8 = (bf16[1,1024,1536]{2,1,0:T(8,128)(2,1)S(1)}, bf16[1,1024,1536]{2,1,0:T(8,128)(2,1)}, u32[]{:S(2)}) copy-start(bf16[1,1024,1536]{2,1,0:T(8,128)(2,1)} %param.7) | copy-start | bytes 9437188
  110.8 1.8 copy-start.7
  234.0 5.0 %copy-start.4 = (bf16[4,128,1024]{2,1,0:T(8,128)(2,1)S(1)}, bf16[4,128,1024]{2,1,0:T(8,128)(2,1)}, u32[]{:S(2)}) copy-start(bf16[4,128,1024]{2,1,0:T(8,128)(2,1)} %copy-done.3) | copy-start | bytes 3145732
